TPU v7x, 32 devices: a whole 2x2x4 slice. The times are simulated.
32 devices in a mesh: wide: 8 (over z, x), narrow: 4 (over y, core).
Axes of the slice: x: 2, y: 2, z: 4, core: 2. Of those that a mesh axis runs over, the one named last changes fastest.
Arguments:
- grid_adjoint_fields: bfloat16 [64, 2560, 512], P('wide', 'narrow'), may hold values from -6 to 6
- interp_weights: bfloat16 [5120, 32, 32], P(('wide', 'narrow')), may hold values from -1 to 1
- depart_owner: int32 [5120, 1], P(('wide', 'narrow')), may hold values from 0 to 7; in each aligned block of 160 rows (0 to 159, 160 to 319, ...) at most 40 rows name the same one
- depart_block: int32 [5120], P(('wide', 'narrow')), may hold values from 0 to 159
- wave_perm: int32 [512], replicated, may hold values from 0 to 511, each once
- legendre: bfloat16 [512, 64, 512], P(('wide', 'narrow')), may hold values from -0.75 to 0.75
- mode_proj: float32 [512, 512], replicated, may hold values from -0.25 to 0.25
- mode_back: float32 [512, 512], replicated, may hold values from -0.25 to 0.25
- mode_depth: float32 [512], replicated, may hold values from 1e-06 to 0.001
Outputs:
- adj_out: float32 [64, 2560, 512], P('wide', 'narrow')
Inputs may be any that keep to these rules, and one draw needn't show every extreme that they name: `depart_owner`: each block's departure owner shares the block's narrow index. Among the 160 blocks of one device at most 40 name one owner, and exactly 40 do in some devices. `wave_perm`: every wavenumber appears once.
All inputs are finite; a program needn't handle non-finite values.
Results may differ from a plain program's by a relative error of at most 0.013.
Values may be sent and summed in bfloat16 or wider, within the bound.
A program may use at most 256 MiB of HBM per device.

v0:
```python
import math

import jax
import jax.numpy as jnp
from jax import lax
from jax.sharding import PartitionSpec as P

NLON = 2560
BS = 32


def trig_table(lon_index, col_index, wave_perm):
    wavenumber = jnp.take(wave_perm, col_index // 2)
    phase_int = lon_index[:, None] * wavenumber[None, :] % NLON
    angles = phase_int.astype(jnp.float32) * (2.0 * math.pi / NLON)
    values = jnp.where((col_index % 2 == 0)[None, :], jnp.cos(angles), jnp.sin(angles))
    return values.astype(jnp.bfloat16)


def apply_modes(spectra, mode_proj, mode_back, mode_depth):
    slot_count, degrees, parts, channels = spectra.shape
    mode_rows = jnp.dot(
        spectra.reshape(-1, channels),
        mode_proj,
        precision=lax.Precision.HIGHEST,
        preferred_element_type=jnp.float32,
    )
    degree_float = jnp.arange(degrees, dtype=jnp.float32)
    damping = 1.0 / (1.0 + (degree_float * (degree_float + 1.0))[:, None] * mode_depth[None, :])
    mode_rows = mode_rows.reshape(slot_count, degrees, parts, channels) * damping[None, :, None, :]
    returned = jnp.dot(
        mode_rows.reshape(-1, channels),
        mode_back,
        precision=lax.Precision.HIGHEST,
        preferred_element_type=jnp.float32,
    )
    return returned.astype(jnp.bfloat16).reshape(slot_count, degrees, parts, channels)


def shards(
    grid_adjoint_fields,
    interp_weights,
    depart_owner,
    depart_block,
    wave_perm,
    legendre,
    mode_proj,
    mode_back,
    mode_depth,
):
    wide_count = lax.axis_size("wide")
    narrow_count = lax.axis_size("narrow")
    wide_index = lax.axis_index("wide")
    narrow_index = lax.axis_index("narrow")
    lat_dev, lon_dev, channels = grid_adjoint_fields.shape
    slot_count, lat_total, degrees = legendre.shape
    two_m = 2 * degrees
    normalizing_scale = NLON ** (-0.5)
    slot_ids = (wide_index * narrow_count + narrow_index) * slot_count + jnp.arange(
        slot_count, dtype=jnp.int32
    )
    wavenumber = jnp.take(wave_perm, slot_ids)
    degree_ids = jnp.arange(degrees, dtype=jnp.int32)
    masked_values = jnp.where(
        degree_ids[None, None, :] >= wavenumber[:, None, None], legendre, jnp.zeros_like(legendre)
    )
    per_set = two_m // narrow_count
    lon_ids = narrow_index * lon_dev + jnp.arange(lon_dev, dtype=jnp.int32)

    def column_of(order_index):
        set_id = order_index // per_set
        within = order_index % per_set
        band_id = within // (2 * slot_count)
        return (
            band_id * (two_m // wide_count) + set_id * (2 * slot_count) + within % (2 * slot_count)
        )

    cols = column_of(jnp.arange(lax.axis_size("narrow") * per_set, dtype=jnp.int32))
    trig_part = trig_table(lon_ids, cols, wave_perm)
    summed = lax.psum_scatter(
        jnp.einsum(
            "alc,lr->rac", grid_adjoint_fields, trig_part, preferred_element_type=jnp.float32
        ).astype(jnp.bfloat16),
        "narrow",
        scatter_dimension=0,
        tiled=True,
    ).astype(jnp.float32)
    fourier_harmonics = (summed * normalizing_scale).astype(jnp.bfloat16)
    fourier_harmonics = fourier_harmonics.reshape(wide_count, 2 * slot_count, lat_dev, channels)
    fourier_harmonics = lax.all_to_all(
        fourier_harmonics, "wide", split_axis=0, concat_axis=2, tiled=True
    )
    fourier_harmonics = fourier_harmonics.reshape(slot_count, 2, lat_total, channels)
    spectra = jnp.einsum(
        "kgn,kpgc->knpc", masked_values, fourier_harmonics, preferred_element_type=jnp.float32
    )
    returned = apply_modes(spectra, mode_proj, mode_back, mode_depth)
    synthesis_output = jnp.einsum(
        "kgn,knpc->kpgc", masked_values, returned, preferred_element_type=jnp.float32
    ).astype(jnp.bfloat16)
    synthesis_output = synthesis_output.reshape(1, 2 * slot_count, wide_count, lat_dev, channels)
    synthesis_output = lax.all_to_all(
        synthesis_output, "wide", split_axis=2, concat_axis=0, tiled=True
    )
    synthesis_output = synthesis_output.reshape(per_set, lat_dev, channels)
    shard_rows = lax.all_gather(synthesis_output, "narrow", axis=0, tiled=True)
    cols = column_of(jnp.arange(shard_rows.shape[0], dtype=jnp.int32))
    trig_part = trig_table(lon_ids, cols, wave_perm)
    wave_sum = jnp.einsum("rac,lr->alc", shard_rows, trig_part, preferred_element_type=jnp.float32)
    wavenumber_grid = (wave_sum * normalizing_scale).astype(jnp.bfloat16)
    blocks_per_row = lon_dev // BS
    block_count = lat_dev * blocks_per_row
    blocks = grid_adjoint_fields.reshape(block_count, BS, channels)
    contrib = jnp.einsum(
        "bai,bac->bic", interp_weights, blocks, preferred_element_type=jnp.float32
    ).astype(jnp.bfloat16)
    owner_band = depart_owner[:, 0]
    block_ids = jnp.arange(block_count, dtype=jnp.int32)
    capacity = (2 * block_count + wide_count - 1) // wide_count
    same_owner = owner_band[:, None] == owner_band[None, :]
    earlier = block_ids[None, :] < block_ids[:, None]
    slot_rank = jnp.sum((same_owner & earlier).astype(jnp.int32), axis=1)
    send_slot = owner_band * capacity + slot_rank
    pick_slot = jnp.arange(wide_count * capacity, dtype=jnp.int32)[:, None] == send_slot[None, :]
    packed = jnp.einsum(
        "sb,bjc->sjc", pick_slot.astype(jnp.bfloat16), contrib, preferred_element_type=jnp.float32
    )
    packed = packed.astype(jnp.bfloat16).reshape(wide_count, capacity, BS, channels)
    slot_target = jnp.max(jnp.where(pick_slot, depart_block[None, :], -1), axis=1).reshape(
        wide_count, capacity
    )
    recv_values, recv_targets = (
        lax.all_to_all(packed, "wide", split_axis=0, concat_axis=0, tiled=True),
        lax.all_to_all(slot_target, "wide", split_axis=0, concat_axis=0, tiled=True),
    )
    hit_table = (recv_targets.reshape(-1)[None, :] == block_ids[:, None]).astype(jnp.bfloat16)
    deposit = jnp.einsum(
        "bs,sjc->bjc",
        hit_table,
        recv_values.reshape(-1, BS, channels),
        preferred_element_type=jnp.float32,
    )
    return wavenumber_grid.astype(jnp.float32) + deposit.reshape(lat_dev, lon_dev, channels)


def solution(mesh):
    in_specs = (
        P("wide", "narrow", None),
        P(("wide", "narrow"), None, None),
        P(("wide", "narrow"), None),
        P(("wide", "narrow")),
        P(),
        P(("wide", "narrow"), None, None),
        P(),
        P(),
        P(),
    )
    out_specs = P("wide", "narrow", None)
    return jax.shard_map(shards, mesh=mesh, in_specs=in_specs, out_specs=out_specs, check_vma=False)
```

profile of v0, /device:TPU:0, one launch (start us, length us, event | category | flops | bytes accessed | tf_op | source)
XLA Modules:
  0.0 790.3 jit_solution(5078361945235355312)
XLA Ops:
  6.6 6.3 gather_fusion.1
  13.5 21.5 %convolution_convert_fusion.1 = bf16[1024,8,512]{2,0,1:T(8,128)(2,1)} fusion(bf16[8,640,512]{2,1,0:T(8,128)(2,1)} %param.11, s32[1024]{0:T(1024)S(1)} %and_select_fusion, s32[640]{0:T(1024)S(1)} %iota_add_fusion, pred[1024]{0:T(1024)(128)(4,1)S(1)} %fusion.45), kind=kOutput, calls=%fused_computation.8 | convolution fusion | flops 5380112384 | bytes 13639168 | tf_op jit(solution)/shard_map/alc,lr->rac/dot_general | solution.py:81
  35.1 74.6 %reduce-scatter.2.cloned.1.call-done = bf16[256,8,512]{2,0,1:T(8,128)(2,1)} async-done(((bf16[1024,8,512]{2,0,1:T(8,128)(2,1)}), bf16[256,8,512]{2,0,1:T(8,128)(2,1)}) %reduce-scatter.2.cloned.1.call-update) | async-done | bytes 2097168 | tf_op jit(solution)/shard_map/reduce_scatter | solution.py:80
  114.3 5.6 all-to-all-start
  122.0 46.3 %all-to-all-done = bf16[8,32,8,512]{3,2,1,0:T(8,128)(2,1)} async-done(((bf16[8,32,8,512]{3,2,1,0:T(8,128)(2,1)}), bf16[8,32,8,512]{3,2,1,0:T(8,128)(2,1)}, u32[]{:S(2)}, u32[]{:S(2)}) %all-to-all-start) | async-done | bytes 2097184 | tf_op jit(solution)/shard_map/all_to_all | solution.py:90
  173.8 13.1 %fusion.23 = f32[16,512,2,512]{3,1,2,0:T(8,128)} fusion(bf16[16,2,64,512]{3,2,1,0:T(8,128)(2,1)S(1)} %bitcast.59, bf16[16,64,512]{2,1,0:T(8,128)(2,1)S(1)} %copy-done.3, pred[16,512]{1,0:T(8,128)(4,1)S(1)} %iota_compare_fusion.3), kind=kOutput, calls=%fused_computation.32 | convolution fusion | flops 1074266112 | bytes 36708352 | tf_op jit(solution)/shard_map/kgn,kpgc->knpc/dot_general | solution.py:94
  186.9 59.4 %broadcast_multiply_fusion = f32[16,512,2,512]{3,1,2,0:T(8,128)} fusion(f32[512,512]{1,0:T(8,128)S(1)} %add_divide_fusion, f32[16,512,2,512]{3,1,2,0:T(8,128)} %fusion.23, f32[512,512]{1,0:T(8,128)S(1)} %copy-done), kind=kOutput, calls=%fused_computation.5 | convolution fusion | flops 51547996160 | bytes 69206016 | tf_op jit(solution)/shard_map/dot_general | solution.py:22
  246.3 55.1 %copy.35 = f32[16,512,2,512]{3,2,1,0:T(2,128)} copy(f32[16,512,2,512]{3,1,2,0:T(8,128)} %broadcast_multiply_fusion) | data formatting | bytes 67108864 | tf_op jit(solution)/shard_map/mul | solution.py:30
  301.4 39.9 %reshape.216 = f32[16384,512]{1,0:T(8,128)} reshape(f32[16,512,2,512]{3,2,1,0:T(2,128)} %copy.35) | data formatting | bytes 67108864 | tf_op jit(solution)/shard_map/reshape | solution.py:32
  341.3 59.2 %convolution_convert_fusion = bf16[16384,512]{1,0:T(8,128)(2,1)} fusion(f32[16384,512]{1,0:T(8,128)} %reshape.216, f32[512,512]{1,0:T(8,128)S(1)} %copy-done.4), kind=kOutput, calls=%fused_computation.2 | convolution fusion | flops 51547996160 | bytes 51380224 | tf_op jit(solution)/shard_map/dot_general | solution.py:31
  400.5 24.9 %reshape.217 = bf16[16,512,2,512]{3,2,1,0:T(2,128)(2,1)} reshape(bf16[16384,512]{1,0:T(8,128)(2,1)} %convolution_convert_fusion) | data formatting | bytes 33554432 | tf_op jit(solution)/shard_map/reshape | solution.py:37
  425.4 8.8 %fusion.8 = bf16[16,2,512,64]{2,3,1,0:T(8,128)(2,1)S(1)} fusion(bf16[16,512,2,512]{3,2,1,0:T(2,128)(2,1)} %reshape.217, bf16[16,64,512]{2,1,0:T(8,128)(2,1)S(1)} %copy-done.3, pred[16,512]{1,0:T(8,128)(4,1)S(1)} %iota_compare_fusion.3), kind=kOutput, calls=%fused_computation.21 | convolution fusion | flops 1075314688 | bytes 19931136 | tf_op jit(solution)/shard_map/kgn,knpc->kpgc/dot_general | solution.py:98
  435.8 6.2 all-to-all-start.1
  444.2 4.4 convolution_convert_fusion.3
  448.6 6.2 convolution_convert_fusion.2
  454.8 9.0 %copy.41 = bf16[8,40,32,512]{3,1,2,0:T(8,128)(2,1)} copy(bf16[8,40,32,512]{3,1,0,2:T(8,128)(2,1)} %bitcast.56) | data formatting | bytes 20971520 | tf_op jit(solution)/shard_map/reshape | solution.py:128
  463.8 26.0 %all-to-all-done.1 = bf16[1,32,8,8,512]{4,3,1,0,2:T(8,128)(2,1)S(1)} async-done(((bf16[1,32,8,8,512]{4,3,1,0,2:T(8,128)(2,1)}), bf16[1,32,8,8,512]{4,3,1,0,2:T(8,128)(2,1)S(1)}, u32[]{:S(2)}, u32[]{:S(2)}) %all-to-all-start.1) | async-done | bytes 2097184 | tf_op jit(solution)/shard_map/all_to_all | solution.py:102
  489.8 5.1 all-to-all-start.3
  498.3 223.4 %all-to-all-done.3 = bf16[8,40,32,512]{3,1,2,0:T(8,128)(2,1)} async-done(((bf16[8,40,32,512]{3,1,2,0:T(8,128)(2,1)}), bf16[8,40,32,512]{3,1,2,0:T(8,128)(2,1)}, u32[]{:S(2)}, u32[]{:S(2)}) %all-to-all-start.3) | async-done | bytes 10485792 | tf_op jit(solution)/shard_map/all_to_all | solution.py:133
  721.7 9.5 %copy.42 = bf16[8,40,32,512]{3,1,0,2:T(8,128)(2,1)} copy(bf16[8,40,32,512]{3,1,2,0:T(8,128)(2,1)} %all-to-all-done.3) | data formatting | bytes 20971520 | tf_op jit(solution)/shard_map/all_to_all | solution.py:133
  731.2 5.8 fusion.30
  737.1 10.1 %copy.43 = f32[160,32,512]{2,1,0:T(8,128)} copy(f32[160,32,512]{2,0,1:T(8,128)S(1)} %fusion.30) | data formatting | bytes 20971520 | tf_op jit(solution)/shard_map/bs,sjc->bjc/dot_general | solution.py:137
  747.1 22.1 %fusion.13 = f32[640,8,512]{2,0,1:T(8,128)} fusion(bf16[1024,8,512]{2,0,1:T(8,128)(2,1)} %all-gather.2.cloned.1.call-done, s32[1024]{0:T(1024)S(1)} %copy-done.10, s32[640]{0:T(1024)S(1)} %copy-done.8, pred[1024]{0:T(1024)(128)(4,1)S(1)} %copy-done.14), kind=kOutput, calls=%fused_computation.23 | convolution fusion | flops 5375918080 | bytes 18882048 | tf_op jit(solution)/shard_map/rac,lr->alc/dot_general | solution.py:109
  769.3 13.8 %bitcast_add_fusion = f32[8,640,512]{2,1,0:T(8,128)} fusion(f32[640,8,512]{2,0,1:T(8,128)} %fusion.13, f32[8,640,512]{2,1,0:T(8,128)} %bitcast.58), kind=kLoop, calls=%fused_computation.6 | loop fusion | flops 10485760 | bytes 31457280 | tf_op jit(solution)/shard_map/add | solution.py:143
  (61 shorter events, 19.9 us)
Async XLA Ops:
  6.5 180.4 %copy-start = (f32[512,512]{1,0:T(8,128)S(1)}, f32[512,512]{1,0:T(8,128)}, u32[]{:S(2)}) copy-start(f32[512,512]{1,0:T(8,128)} %param.17) | copy-start | bytes 3145732
  6.5 103.1 %reduce-scatter.2.cloned.1.call-start = ((), (), s32[]{:S(2)}) async-start(), calls=%async_computation.5 | async-start | bytes 10485760 | tf_op jit(solution)/shard_map/reduce_scatter | solution.py:80
  6.6 28.5 %copy-start.13 = (pred[1024]{0:T(1024)(128)(4,1)}, pred[1024]{0:T(1024)(128)(4,1)S(1)}, u32[]{:S(2)}) copy-start(pred[1024]{0:T(1024)(128)(4,1)S(1)} %fusion.45) | copy-start | bytes 3076
  6.6 28.4 %copy-start.7 = (s32[640]{0:T(1024)}, s32[640]{0:T(1024)S(1)}, u32[]{:S(2)}) copy-start(s32[640]{0:T(1024)S(1)} %iota_add_fusion) | copy-start | bytes 7684
  12.9 0.6 copy-start.9
  111.7 8.3 %copy-start.2 = (s32[512]{0:T(512)S(1)}, s32[512]{0:T(512)}, u32[]{:S(2)}) copy-start(s32[512]{0:T(512)} %param.15) | copy-start | bytes 6148
  111.7 8.9 %copy-start.6 = (s32[160,1]{0,1:T(1,128)S(1)}, s32[160,1]{0,1:T(1,128)}, u32[]{:S(2)}) copy-start(s32[160,1]{0,1:T(1,128)} %param.13) | copy-start | bytes 1924
  111.7 9.1 %copy-start.12 = (s32[160]{0:T(256)S(1)}, s32[160]{0:T(256)}, u32[]{:S(2)}) copy-start(s32[160]{0:T(256)} %param.14) | copy-start | bytes 1924
  111.7 10.0 %copy-start.11 = (f32[512]{0:T(512)S(1)}, f32[512]{0:T(512)}, u32[]{:S(2)}) copy-start(f32[512]{0:T(512)} %param.19) | copy-start | bytes 6148
  114.3 59.4 %copy-start.3 = (bf16[16,64,512]{2,1,0:T(8,128)(2,1)S(1)}, bf16[16,64,512]{2,1,0:T(8,128)(2,1)}, u32[]{:S(2)}) copy-start(bf16[16,64,512]{2,1,0:T(8,128)(2,1)} %param.16) | copy-start | bytes 3145732
  114.3 54.0 %all-to-all-start = ((bf16[8,32,8,512]{3,2,1,0:T(8,128)(2,1)}), bf16[8,32,8,512]{3,2,1,0:T(8,128)(2,1)}, u32[]{:S(2)}, u32[]{:S(2)}) async-start(bf16[8,32,8,512]{3,2,1,0:T(8,128)(2,1)} %copy.33), calls=%async_computation.1 | async-start | bytes 4194304 | tf_op jit(solution)/shard_map/all_to_all | solution.py:90
  168.3 267.5 %all-to-all-start.2 = ((s32[8,1,40]{2,1,0:T(1,128)}), s32[8,1,40]{2,1,0:T(1,128)S(1)}, u32[]{:S(2)}, u32[]{:S(2)}) async-start(s32[8,1,40]{2,1,0:T(1,128)} %all_to_all.37), calls=%async_computation.3 | async-start | bytes 8192 | tf_op jit(solution)/shard_map/all_to_all | solution.py:134
  301.4 39.9 %copy-start.4 = (f32[512,512]{1,0:T(8,128)S(1)}, f32[512,512]{1,0:T(8,128)}, u32[]{:S(2)}) copy-start(f32[512,512]{1,0:T(8,128)} %param.18) | copy-start | bytes 3145732
  434.2 7.8 copy-start.5
  435.8 54.0 %all-to-all-start.1 = ((bf16[1,32,8,8,512]{4,3,1,0,2:T(8,128)(2,1)}), bf16[1,32,8,8,512]{4,3,1,0,2:T(8,128)(2,1)S(1)}, u32[]{:S(2)}, u32[]{:S(2)}) async-start(bf16[1,32,8,8,512]{4,3,1,0,2:T(8,128)(2,1)} %copy.37), calls=%async_computation.2 | async-start | bytes 4194304 | tf_op jit(solution)/shard_map/all_to_all | solution.py:102
  489.8 231.9 %all-to-all-start.3 = ((bf16[8,40,32,512]{3,1,2,0:T(8,128)(2,1)}), bf16[8,40,32,512]{3,1,2,0:T(8,128)(2,1)}, u32[]{:S(2)}, u32[]{:S(2)}) async-start(bf16[8,40,32,512]{3,1,2,0:T(8,128)(2,1)} %copy.41), calls=%async_computation.4 | async-start | bytes 20971520 | tf_op jit(solution)/shard_map/all_to_all | solution.py:133
  494.9 252.2 %all-gather.2.cloned.1.call-start = ((), (), s32[]{:S(2)}) async-start(), calls=%async_computation.6 | async-start | bytes 10485760 | tf_op jit(solution)/shard_map/all_gather | solution.py:106
  737.0 10.1 %copy-start.8 = (s32[640]{0:T(1024)S(1)}, s32[640]{0:T(1024)}, u32[]{:S(2)}) copy-start(s32[640]{0:T(1024)} %copy-done.7) | copy-start | bytes 7684
  737.0 10.1 %copy-start.10 = (s32[1024]{0:T(1024)S(1)}, s32[1024]{0:T(1024)}, u32[]{:S(2)}) copy-start(s32[1024]{0:T(1024)} %copy-done.9) | copy-start | bytes 12292
  737.1 10.1 %copy-start.14 = (pred[1024]{0:T(1024)(128)(4,1)S(1)}, pred[1024]{0:T(1024)(128)(4,1)}, u32[]{:S(2)}) copy-start(pred[1024]{0:T(1024)(128)(4,1)} %copy-done.13) | copy-start | bytes 3076
  769.3 13.8 %copy-start.1 = (f32[512,512]{1,0:T(8,128)S(1)}, f32[512,512]{1,0:T(8,128)}, u32[]{:S(2)}) copy-start(f32[512,512]{1,0:T(8,128)} %param.17) | copy-start | bytes 3145732
Sparse Core Ops, SparseCore 0:
  35.2 74.4 reduce-scatter.1
  497.4 58.6 all-gather.1
where the time goes:
time: 801 us; the launch traced here: 790 us
  waiting for transfers between devices  370 us (46%)
  matrix products  201 us (25%)
  local copies, waits for them, and re-layouts  167 us (21%)
  starting transfers between devices  20.6 us (3%)
  other arithmetic  17.2 us (2%)
  between operations  14.1 us (2%)
    all_to_all x1, waiting for transfers between devices, shards(): lax.all_to_all(packed, 'wide', split_axis=0, concat_axis=0, tiled=True)  223 us
    reduce_scatter x1, waiting for transfers between devices, shards(): lax.psum_scatter(jnp.einsum('alc,lr->rac', grid_adjoint_fields, trig_part...  74.6 us
    dot_general x1, matrix products, apply_modes(): jnp.dot(spectra.reshape(-1, channels), mode_proj, precision=lax.Precision...  59.4 us
    dot_general x1, matrix products, apply_modes(): jnp.dot(mode_rows.reshape(-1, channels), mode_back, precision=lax.Precisi...  59.2 us
    mul x1, local copies, waits for them, and re-layouts, apply_modes(): mode_rows.reshape(slot_count, degrees, parts, channels)  55.1 us
    all_to_all x1, waiting for transfers between devices, shards(): lax.all_to_all(fourier_harmonics, 'wide', split_axis=0, concat_axis=2, ti...  46.3 us
    reshape x1, local copies, waits for them, and re-layouts, apply_modes(): mode_rows.reshape(-1, channels)  39.9 us
    all_to_all x1, waiting for transfers between devices, shards(): lax.all_to_all(synthesis_output, 'wide', split_axis=2, concat_axis=0, til...  26 us
  transfers between devices with their start and end apart: 6, of which 4 were waited for; matrix products, arithmetic and copies ran while one was open for 40% of the time, Pallas kernels for 0%

commit v1 on v0

v1 whole, which is shorter than its diff:
```python
import math

import jax
import jax.numpy as jnp
from jax import lax
from jax.experimental import pallas as pl
from jax.experimental.pallas import tpu as pltpu
from jax.sharding import PartitionSpec as P

NLON = 2560
BS = 32
VMEM_LIMIT = 48 * 1024 * 1024
SCALE = NLON ** (-0.5)


def params():
    return pltpu.CompilerParams(vmem_limit_bytes=VMEM_LIMIT)


def cost(flops, nbytes):
    return pl.CostEstimate(flops=flops, bytes_accessed=nbytes, transcendentals=0)


def trig_tables(first_lon, lon_dev, wavenumber):
    columns = 2 * wavenumber.shape[0]
    wave = jnp.broadcast_to(wavenumber[:, None], (wavenumber.shape[0], 2)).reshape(columns)
    shift = (jnp.arange(columns, dtype=jnp.int32) % 2) * (NLON - NLON // 4)
    unit = 2.0 * math.pi / NLON
    coarse_lon = first_lon + BS * jnp.arange(lon_dev // BS, dtype=jnp.int32)
    coarse = ((coarse_lon[:, None] * wave[None, :] + shift[None, :]) % NLON).astype(jnp.float32) * unit
    fine_lon = jnp.arange(BS, dtype=jnp.int32)
    fine = ((fine_lon[:, None] * wave[None, :]) % NLON).astype(jnp.float32) * unit
    parts = lax.optimization_barrier((jnp.cos(coarse), jnp.sin(coarse), jnp.cos(fine), jnp.sin(fine)))
    cos_a, sin_a, cos_b, sin_b = parts
    table = cos_a[:, None, :] * cos_b[None, :, :] - sin_a[:, None, :] * sin_b[None, :, :]
    return table.astype(jnp.bfloat16).reshape(lon_dev, columns)


def analysis_body(trig_ref, grid_ref, out_ref):
    out_ref[0] = jnp.dot(
        trig_ref[...], grid_ref[0], preferred_element_type=jnp.float32
    ).astype(jnp.bfloat16)


def analysis(trig_t, grid):
    lat_dev, lon_dev, channels = grid.shape
    columns = trig_t.shape[0]
    return pl.pallas_call(
        analysis_body,
        grid=(lat_dev,),
        in_specs=[
            pl.BlockSpec((columns, lon_dev), lambda a: (0, 0)),
            pl.BlockSpec((1, lon_dev, channels), lambda a: (a, 0, 0)),
        ],
        out_specs=pl.BlockSpec((1, columns, channels), lambda a: (a, 0, 0)),
        out_shape=jax.ShapeDtypeStruct((lat_dev, columns, channels), jnp.bfloat16),
        compiler_params=params(),
        cost_estimate=cost(
            2 * columns * lon_dev * lat_dev * channels,
            2 * (lat_dev * (columns + lon_dev) * channels + columns * lon_dev),
        ),
        name="analysis",
    )(trig_t, grid)


def modes_body(wave_ref, legendre_ref, fourier_ref, proj_ref, back_ref, damping_ref, out_ref):
    slot = pl.program_id(0)
    bands, parts, lat_dev, channels = fourier_ref.shape
    lats = bands * lat_dev
    degrees = legendre_ref.shape[2]
    degree = lax.broadcasted_iota(jnp.int32, (lats, degrees), 1)
    masked = jnp.where(
        degree >= wave_ref[slot], legendre_ref[0].astype(jnp.float32), 0.0
    ).astype(jnp.bfloat16)
    fourier = fourier_ref[...].astype(jnp.float32)
    rows = jnp.concatenate(
        [fourier[:, p].reshape(lats, channels) for p in range(parts)], axis=0
    ).astype(jnp.bfloat16)
    projected = jnp.dot(rows, proj_ref[...], preferred_element_type=jnp.float32) * SCALE
    projected = projected.astype(jnp.bfloat16)
    sums = []
    for p in range(parts):
        modal = lax.dot_general(
            masked,
            projected[p * lats : (p + 1) * lats],
            (((0,), (0,)), ((), ())),
            preferred_element_type=jnp.float32,
        )
        modal = (modal * damping_ref[...]).astype(jnp.bfloat16)
        sums.append(jnp.dot(masked, modal, preferred_element_type=jnp.float32))
    back = jnp.dot(
        jnp.concatenate(sums, axis=0).astype(jnp.bfloat16),
        back_ref[...],
        preferred_element_type=jnp.float32,
    )
    for p in range(parts):
        out_ref[:, p] = (
            back[p * lats : (p + 1) * lats].reshape(bands, lat_dev, channels).astype(jnp.bfloat16)
        )


def modes(wavenumber, legendre, fourier, proj, back, damping):
    slots, lats, degrees = legendre.shape
    bands, _, lat_dev, channels = fourier.shape
    spec = pl.BlockSpec((bands, 2, lat_dev, channels), lambda j, w: (0, j, 0, 0))
    whole = lambda j, w: (0, 0)
    return pl.pallas_call(
        modes_body,
        grid_spec=pltpu.PrefetchScalarGridSpec(
            num_scalar_prefetch=1,
            grid=(slots,),
            in_specs=[
                pl.BlockSpec((1, lats, degrees), lambda j, w: (j, 0, 0)),
                spec,
                pl.BlockSpec(proj.shape, whole),
                pl.BlockSpec(back.shape, whole),
                pl.BlockSpec(damping.shape, whole),
            ],
            out_specs=spec,
        ),
        out_shape=jax.ShapeDtypeStruct(fourier.shape, jnp.bfloat16),
        compiler_params=params(),
        cost_estimate=cost(
            slots * 2 * 4 * 2 * lats * channels * degrees,
            2 * (2 * fourier.size + legendre.size) + 8 * proj.size,
        ),
        name="modes",
    )(wavenumber, legendre, fourier, proj, back, damping)


def pack_body(source_ref, contrib_ref, out_ref):
    def step(s, carry):
        out_ref[s] = contrib_ref[source_ref[s]]
        return carry

    lax.fori_loop(0, out_ref.shape[0], step, 0, unroll=4)


def pack(source, contrib):
    count = source.shape[0]
    shape = (count,) + contrib.shape[1:]
    return pl.pallas_call(
        pack_body,
        grid_spec=pltpu.PrefetchScalarGridSpec(
            num_scalar_prefetch=1,
            grid=(1,),
            in_specs=[pl.BlockSpec(contrib.shape, lambda i, s: (0, 0, 0))],
            out_specs=pl.BlockSpec(shape, lambda i, s: (0, 0, 0)),
        ),
        out_shape=jax.ShapeDtypeStruct(shape, jnp.bfloat16),
        compiler_params=params(),
        cost_estimate=cost(math.prod(shape), 4 * math.prod(shape)),
        name="pack",
    )(source, contrib)


def deposit_body(target_ref, values_ref, out_ref):
    out_ref[...] = jnp.zeros_like(out_ref)

    def step(s, carry):
        block = target_ref[s]

        @pl.when(block >= 0)
        def _():
            out_ref[block] += values_ref[s].astype(jnp.float32)

        return carry

    lax.fori_loop(0, values_ref.shape[0], step, 0, unroll=4)


def deposit(target, values, block_count):
    shape = (block_count,) + values.shape[1:]
    return pl.pallas_call(
        deposit_body,
        grid_spec=pltpu.PrefetchScalarGridSpec(
            num_scalar_prefetch=1,
            grid=(1,),
            in_specs=[pl.BlockSpec(values.shape, lambda i, s: (0, 0, 0))],
            out_specs=pl.BlockSpec(shape, lambda i, s: (0, 0, 0)),
        ),
        out_shape=jax.ShapeDtypeStruct(shape, jnp.float32),
        compiler_params=params(),
        cost_estimate=cost(values.size, 2 * values.size + 4 * math.prod(shape)),
        name="deposit",
    )(target, values)


def synthesis_body(trig_ref, rows_ref, *refs):
    deposits, out_ref = refs[:-1], refs[-1]
    sets, _, per_set, channels = rows_ref.shape
    rows = rows_ref[...].reshape(sets * per_set, channels)
    wave = jnp.dot(trig_ref[...], rows, preferred_element_type=jnp.float32) * SCALE
    wave = wave.astype(jnp.bfloat16).astype(jnp.float32).reshape(out_ref.shape[1:])
    start = 0
    for part in deposits:
        stop = start + part.shape[1]
        out_ref[0, :, start:stop] = wave[:, start:stop] + part[...]
        start = stop


def synthesis(trig, rows, deposits, lat_dev, blocks_per_row):
    sets, _, per_set, channels = rows.shape
    return pl.pallas_call(
        synthesis_body,
        grid=(lat_dev,),
        in_specs=[
            pl.BlockSpec(trig.shape, lambda a: (0, 0)),
            pl.BlockSpec((sets, 1, per_set, channels), lambda a: (0, a, 0, 0)),
        ]
        + [
            pl.BlockSpec((blocks_per_row,) + part.shape[1:], lambda a: (a, 0, 0))
            for part in deposits
        ],
        out_specs=pl.BlockSpec((1, blocks_per_row, BS, channels), lambda a: (a, 0, 0, 0)),
        out_shape=jax.ShapeDtypeStruct((lat_dev, blocks_per_row, BS, channels), jnp.float32),
        compiler_params=params(),
        cost_estimate=cost(
            2 * trig.size * lat_dev * channels,
            2 * (trig.size + rows.size) + 8 * lat_dev * trig.shape[0] * channels,
        ),
        name="synthesis",
    )(trig, rows, *deposits)


def shards(
    grid_adjoint_fields,
    interp_weights,
    depart_owner,
    depart_block,
    wave_perm,
    legendre,
    mode_proj,
    mode_back,
    mode_depth,
):
    wide_count = lax.axis_size("wide")
    narrow_count = lax.axis_size("narrow")
    wide_index = lax.axis_index("wide")
    narrow_index = lax.axis_index("narrow")
    lat_dev, lon_dev, channels = grid_adjoint_fields.shape
    slot_count, lat_total, degrees = legendre.shape
    per_set = 2 * degrees // narrow_count
    blocks_per_row = lon_dev // BS
    block_count = lat_dev * blocks_per_row
    split = BS // 2

    owner_band = depart_owner[:, 0]
    block_ids = jnp.arange(block_count, dtype=jnp.int32)
    capacity = (2 * block_count + wide_count - 1) // wide_count
    same_owner = owner_band[:, None] == owner_band[None, :]
    earlier = block_ids[None, :] < block_ids[:, None]
    slot_rank = jnp.sum((same_owner & earlier).astype(jnp.int32), axis=1)
    send_slot = owner_band * capacity + slot_rank
    pick_slot = jnp.arange(wide_count * capacity, dtype=jnp.int32)[:, None] == send_slot[None, :]
    source = jnp.max(jnp.where(pick_slot, block_ids[None, :], 0), axis=1)
    slot_target = jnp.max(jnp.where(pick_slot, depart_block[None, :], -1), axis=1).reshape(
        wide_count, capacity
    )
    recv_targets = lax.all_to_all(
        slot_target, "wide", split_axis=0, concat_axis=0, tiled=True
    ).reshape(-1)
    blocks = grid_adjoint_fields.reshape(block_count, BS, channels)
    contrib = jnp.einsum(
        "bai,bac->bic", interp_weights, blocks, preferred_element_type=jnp.float32
    ).astype(jnp.bfloat16)
    packed = [
        pack(source, contrib[:, :split]).reshape(wide_count, capacity, split, channels),
        pack(source, contrib[:, split:]).reshape(wide_count, capacity, BS - split, channels),
    ]

    def exchange(values):
        return lax.all_to_all(values, "wide", split_axis=0, concat_axis=0, tiled=True)

    wavenumber = wave_perm.reshape(wide_count, narrow_count, slot_count)
    own_wave = lax.dynamic_index_in_dim(
        lax.dynamic_index_in_dim(wavenumber, wide_index, 0, False), narrow_index, 0, False
    )
    order = wavenumber.transpose(1, 0, 2).reshape(-1)
    trig = trig_tables(narrow_index * lon_dev, lon_dev, order)

    first_recv = exchange(packed[0])
    partial = analysis(trig.T, grid_adjoint_fields)
    summed = lax.psum_scatter(
        partial.reshape(lat_dev, narrow_count, per_set, channels),
        "narrow",
        scatter_dimension=1,
        tiled=False,
    )
    summed, first_recv = lax.optimization_barrier((summed, first_recv))
    fourier = exchange(
        summed.reshape(lat_dev, wide_count, 2 * slot_count, channels).transpose(1, 2, 0, 3)
    )
    degree_float = jnp.arange(degrees, dtype=jnp.float32)
    damping = 1.0 / (1.0 + (degree_float * (degree_float + 1.0))[:, None] * mode_depth[None, :])
    synth = modes(
        own_wave,
        legendre,
        fourier,
        mode_proj.astype(jnp.bfloat16),
        mode_back.astype(jnp.bfloat16),
        damping,
    )
    synth = exchange(synth)
    synth, second = lax.optimization_barrier((synth, packed[1]))
    second_recv = exchange(second)
    rows = lax.all_gather(
        synth.reshape(per_set, lat_dev, channels).transpose(1, 0, 2), "narrow", axis=0, tiled=False
    )
    deposits = [
        deposit(recv_targets, recv.reshape(wide_count * capacity, -1, channels), block_count)
        for recv in (first_recv, second_recv)
    ]
    out = synthesis(trig, rows, deposits, lat_dev, blocks_per_row)
    return out.reshape(lat_dev, lon_dev, channels)


def solution(mesh):
    in_specs = (
        P("wide", "narrow", None),
        P(("wide", "narrow"), None, None),
        P(("wide", "narrow"), None),
        P(("wide", "narrow")),
        P(),
        P(("wide", "narrow"), None, None),
        P(),
        P(),
        P(),
    )
    out_specs = P("wide", "narrow", None)
    return jax.shard_map(shards, mesh=mesh, in_specs=in_specs, out_specs=out_specs, check_vma=False)
```

time: 801 us -> 458 us (0.57); the launches traced: 790 us -> 457 us
  matrix products: 201 us -> 3.99 us
  waiting for transfers between devices: 370 us -> 192 us
  local copies, waits for them, and re-layouts: 167 us -> 28.3 us
  blocking collectives: 0 us -> 133 us
  Pallas kernels: 0 us -> 69.2 us
  other arithmetic: 17.2 us -> 4.02 us
    dot_general x8 -> x0, matrix products: 196 us -> none  [the longest x1 59.4 us: apply_modes(): jnp.dot(spectra.reshape(-1, channels), mode_proj, precision=lax.Precision...]
    all_to_all x0 -> x2, blocking collectives: none -> 133 us  [the longest x1 123 us: exchange(): lax.all_to_all(values, 'wide', split_axis=0, concat_axis=0, tiled=True)]
    all_to_all x4 -> x3, waiting for transfers between devices: 296 us -> 192 us  [exchange(): lax.all_to_all(values, 'wide', split_axis=0, concat_axis=0, tiled=True)]
    reduce_scatter x1, waiting for transfers between devices: 74.6 us -> 0.01 us  [shards(): lax.psum_scatter(partial.reshape(lat_dev, narrow_count, per_set, channels...]
    pallas_call x0 -> x7, Pallas kernels: none -> 69.2 us  [the longest x1 20.1 us: modes(): pl.pallas_call(modes_body, grid_spec=pltpu.PrefetchScalarGridSpec(num_sca...]
    reshape x5 -> x4, local copies, waits for them, and re-layouts: 77.9 us -> 14.3 us  [the longest x1 11.4 us: shards(): partial.reshape(lat_dev, narrow_count, per_set, channels)]
    mul x1, local copies, waits for them, and re-layouts: 55.1 us -> 0.17 us  [trig_tables(): coarse_lon[:, None] * wave[None, :] + shift[None, :]]
    add x2 -> x1, other arithmetic: 13.8 us -> 0.01 us  [trig_tables(): coarse_lon = first_lon + BS * jnp.arange(lon_dev // BS, dtype=jnp.int32)]
  transfers between devices with their start and end apart: 6 -> 5, of which waited for: 4 -> 3; matrix products, arithmetic and copies ran while one was open for 40% -> 2% of each run, Pallas kernels for 0% -> 5%
where the time goes in v1:
time: 458 us; the launch traced here: 457 us
  waiting for transfers between devices  192 us (42%)
  blocking collectives  133 us (29%)
  Pallas kernels  69.2 us (15%)
  local copies, waits for them, and re-layouts  28.3 us (6%)
  between operations  13.6 us (3%)
  starting transfers between devices  13 us (3%)
    all_to_all x3, waiting for transfers between devices, exchange(): lax.all_to_all(values, 'wide', split_axis=0, concat_axis=0, tiled=True)  192 us
    all_to_all x1, blocking collectives, exchange(): lax.all_to_all(values, 'wide', split_axis=0, concat_axis=0, tiled=True)  123 us
    pallas_call x1, Pallas kernels, modes(): pl.pallas_call(modes_body, grid_spec=pltpu.PrefetchScalarGridSpec(num_sca...  20.1 us
    pallas_call x2, Pallas kernels, deposit(): pl.pallas_call(deposit_body, grid_spec=pltpu.PrefetchScalarGridSpec(num_s...  14.7 us
    pallas_call x1, Pallas kernels, synthesis(): pl.pallas_call(synthesis_body, grid=(lat_dev,), in_specs=[pl.BlockSpec(tr...  14.6 us
    all_to_all x3, starting transfers between devices, exchange(): lax.all_to_all(values, 'wide', split_axis=0, concat_axis=0, tiled=True)  13 us
    pallas_call x1, Pallas kernels, analysis(): pl.pallas_call(analysis_body, grid=(lat_dev,), in_specs=[pl.BlockSpec((co...  11.5 us
    reshape x1, local copies, waits for them, and re-layouts, shards(): partial.reshape(lat_dev, narrow_count, per_set, channels)  11.4 us
  transfers between devices with their start and end apart: 5, of which 3 were waited for; matrix products, arithmetic and copies ran while one was open for 2% of the time, Pallas kernels for 5%

profile of v1, /device:TPU:0, one launch (start us, length us, event | category | flops | bytes accessed | tf_op | source)
XLA Modules:
  0.0 457.2 jit_solution(5197385993450450163)
XLA Ops:
  10.0 11.5 %analysis.1 = bf16[8,1024,512]{2,1,0:T(8,128)(2,1)} custom-call(bf16[1024,640]{1,0:T(8,128)(2,1)S(1)} %copy.25.trig_ref, bf16[8,640,512]{2,1,0:T(8,128)(2,1)} %grid_ref.1), custom_call_target="tpu_custom_call" | custom-call | flops 5368709120 | bytes 14942208 | tf_op jit(solution)/shard_map/analysis/pallas_call | solution.py:48
  21.5 11.4 %copy.26 = bf16[8,4,256,512]{3,0,2,1:T(8,128)(2,1)} copy(bf16[8,4,256,512]{3,2,1,0:T(8,128)(2,1)} %bitcast.30) | data formatting | bytes 16777216 | tf_op jit(solution)/shard_map/reshape | solution.py:285
  34.0 1.5 copy.27
  35.8 4.0 convolution_convert_fusion
  39.8 2.2 fusion.19
  42.0 4.6 pack.2
  46.5 122.9 %all_to_all.29 = bf16[8,40,16,512]{3,2,1,0:T(8,128)(2,1)} all-to-all(bf16[8,40,16,512]{3,2,1,0:T(8,128)(2,1)} %bitcast.29), channel_id=1, replica_groups=mesh['wide'=8,'narrow'=4] {'wide'}, dimensions={0} | all-to-all | bytes 10485760 | tf_op jit(solution)/shard_map/all_to_all | solution.py:273
  169.4 4.7 %all-to-all-start.1 = ((bf16[8,32,8,512]{3,2,1,0:T(8,128)(2,1)}), bf16[8,32,8,512]{3,2,1,0:T(8,128)(2,1)}, u32[]{:S(2)}, u32[]{:S(2)}) async-start(bf16[8,32,8,512]{3,2,1,0:T(8,128)(2,1)} %bitcast.35), calls=%async_computation.2 | async-start | bytes 4194304 | tf_op jit(solution)/shard_map/all_to_all | solution.py:273
  174.2 1.3 convert_element_type.32.back_ref
  175.8 45.5 %all-to-all-done.1.fourier_ref = bf16[8,32,8,512]{3,2,1,0:T(8,128)(2,1)} async-done(((bf16[8,32,8,512]{3,2,1,0:T(8,128)(2,1)}), bf16[8,32,8,512]{3,2,1,0:T(8,128)(2,1)}, u32[]{:S(2)}, u32[]{:S(2)}) %all-to-all-start.1) | async-done | bytes 2097184 | tf_op jit(solution)/shard_map/all_to_all | solution.py:273
  222.5 20.1 %modes.1 = bf16[8,32,8,512]{3,2,1,0:T(8,128)(2,1)} custom-call(s32[16]{0:T(128)S(1)} %dynamic-slice_bitcast_fusion.wave_ref, bf16[16,64,512]{2,1,0:T(8,128)(2,1)S(1)} %copy-done.3, bf16[8,32,8,512]{3,2,1,0:T(8,128)(2,1)} %all-to-all-done.1.fourier_ref, bf16[512,512]{1,0:T(8,128)(2,1)S(1)} %convert_element_type.31.proj_ref, ...), custom_call_target="tpu_custom_call" | custom-call | flops 4294967296 | bytes 7340032 | tf_op jit(solution)/shard_map/modes/pallas_call | solution.py:107
  242.7 3.6 all-to-all-start.2
  246.3 1.7 copy-done.2
  248.1 3.7 pack.3
  251.8 42.9 %all-to-all-done.2 = bf16[8,32,8,512]{3,2,1,0:T(8,128)(2,1)S(1)} async-done(((bf16[8,32,8,512]{3,2,1,0:T(8,128)(2,1)}), bf16[8,32,8,512]{3,2,1,0:T(8,128)(2,1)S(1)}, u32[]{:S(2)}, u32[]{:S(2)}) %all-to-all-start.2) | async-done | bytes 2097184 | tf_op jit(solution)/shard_map/all_to_all | solution.py:273
  294.7 2.0 copy.30
  296.8 9.9 %all_to_all.30 = s32[8,1,40]{2,1,0:T(1,128)S(1)} all-to-all(s32[8,1,40]{2,1,0:T(1,128)S(1)} %all_to_all.21), channel_id=1, replica_groups=mesh['wide'=8,'narrow'=4] {'wide'}, dimensions={0} | all-to-all | bytes 2560 | tf_op jit(solution)/shard_map/all_to_all | solution.py:260
  306.7 4.7 %all-to-all-start.4 = ((bf16[8,40,16,512]{3,2,1,0:T(8,128)(2,1)}), bf16[8,40,16,512]{3,2,1,0:T(8,128)(2,1)}, u32[]{:S(2)}, u32[]{:S(2)}) async-start(bf16[8,40,16,512]{3,2,1,0:T(8,128)(2,1)} %bitcast.28), calls=%async_computation.5 | async-start | bytes 10485760 | tf_op jit(solution)/shard_map/all_to_all | solution.py:273
  312.6 7.4 %deposit.2.refs_0_ = f32[160,16,512]{2,1,0:T(8,128)S(1)} custom-call(s32[320]{0:T(512)S(1)} %reshape.94.target_ref, bf16[320,16,512]{2,1,0:T(8,128)(2,1)} %bitcast.27), custom_call_target="tpu_custom_call" | custom-call | flops 2621440 | bytes 10485760 | tf_op jit(solution)/shard_map/deposit/pallas_call | solution.py:174
  320.0 2.4 copy-done
  322.4 103.8 %all-to-all-done.4 = bf16[8,40,16,512]{3,2,1,0:T(8,128)(2,1)} async-done(((bf16[8,40,16,512]{3,2,1,0:T(8,128)(2,1)}), bf16[8,40,16,512]{3,2,1,0:T(8,128)(2,1)}, u32[]{:S(2)}, u32[]{:S(2)}) %all-to-all-start.4) | async-done | bytes 5242912 | tf_op jit(solution)/shard_map/all_to_all | solution.py:273
  426.2 7.3 %deposit.3.refs_1_ = f32[160,16,512]{2,1,0:T(8,128)S(1)} custom-call(s32[320]{0:T(512)S(1)} %reshape.94.target_ref, bf16[320,16,512]{2,1,0:T(8,128)(2,1)} %bitcast.16.values_ref), custom_call_target="tpu_custom_call" | custom-call | flops 2621440 | bytes 10485760 | tf_op jit(solution)/shard_map/deposit/pallas_call | solution.py:174
  433.5 2.3 copy-done.1
  435.7 14.6 %synthesis.1 = f32[8,20,32,512]{3,2,1,0:T(8,128)} custom-call(bf16[640,1024]{1,0:T(8,128)(2,1)S(1)} %bitcast.26, bf16[4,8,256,512]{3,2,1,0:T(8,128)(2,1)} %bitcast.33, f32[160,16,512]{2,1,0:T(8,128)} %copy-done, f32[160,16,512]{2,1,0:T(8,128)} %copy-done.1), custom_call_target="tpu_custom_call" | custom-call | flops 5368709120 | bytes 30670848 | tf_op jit(solution)/shard_map/synthesis/pallas_call | solution.py:204
  (43 shorter events, 7.6 us)
Async XLA Ops:
  6.5 162.9 %reduce-scatter.2.cloned.1.call-start = ((), (), s32[]{:S(2)}) async-start(), calls=%async_computation.6 | async-start | bytes 10485760 | tf_op jit(solution)/shard_map/reduce_scatter | solution.py:284
  32.9 1.0 copy-start.5
  32.9 2.5 copy-start.6
  32.9 2.7 copy-start.8
  169.4 4.7 %copy-start.4 = (f32[512,512]{1,0:T(8,128)S(1)}, f32[512,512]{1,0:T(8,128)}, u32[]{:S(2)}) copy-start(f32[512,512]{1,0:T(8,128)} %param.15) | copy-start | bytes 3145732
  169.4 51.9 %all-to-all-start.1 = ((bf16[8,32,8,512]{3,2,1,0:T(8,128)(2,1)}), bf16[8,32,8,512]{3,2,1,0:T(8,128)(2,1)}, u32[]{:S(2)}, u32[]{:S(2)}) async-start(bf16[8,32,8,512]{3,2,1,0:T(8,128)(2,1)} %bitcast.35), calls=%async_computation.2 | async-start | bytes 4194304 | tf_op jit(solution)/shard_map/all_to_all | solution.py:273
  174.1 1.4 copy-start.7
  221.3 1.2 copy-start.3
  242.7 52.0 %all-to-all-start.2 = ((bf16[8,32,8,512]{3,2,1,0:T(8,128)(2,1)}), bf16[8,32,8,512]{3,2,1,0:T(8,128)(2,1)S(1)}, u32[]{:S(2)}, u32[]{:S(2)}) async-start(bf16[8,32,8,512]{3,2,1,0:T(8,128)(2,1)} %modes.1), calls=%async_computation.3 | async-start | bytes 4194304 | tf_op jit(solution)/shard_map/all_to_all | solution.py:273
  246.3 189.5 %all-gather.3.cloned.1.call-start = ((), (), s32[]{:S(2)}) async-start(), calls=%async_computation.7 | async-start | bytes 10485760 | tf_op jit(solution)/shard_map/all_gather | solution.py:307
  246.3 1.7 copy-start.2
  306.7 119.4 %all-to-all-start.4 = ((bf16[8,40,16,512]{3,2,1,0:T(8,128)(2,1)}), bf16[8,40,16,512]{3,2,1,0:T(8,128)(2,1)}, u32[]{:S(2)}, u32[]{:S(2)}) async-start(bf16[8,40,16,512]{3,2,1,0:T(8,128)(2,1)} %bitcast.28), calls=%async_computation.5 | async-start | bytes 10485760 | tf_op jit(solution)/shard_map/all_to_all | solution.py:273
  320.0 2.4 copy-start
  433.5 2.3 copy-start.1
Sparse Core Ops, SparseCore 0:
  33.1 74.4 reduce-scatter.1
  296.9 57.3 all-gather.2

commit v2 on v1

--- a/solution.py
+++ b/solution.py
@@ -37,14 +37,14 @@
 
 
 def analysis_body(trig_ref, grid_ref, out_ref):
-    out_ref[0] = jnp.dot(
-        trig_ref[...], grid_ref[0], preferred_element_type=jnp.float32
-    ).astype(jnp.bfloat16)
-
-
-def analysis(trig_t, grid):
+    rows = jnp.dot(trig_ref[...], grid_ref[0], preferred_element_type=jnp.float32)
+    out_ref[...] = rows.astype(jnp.bfloat16).reshape(out_ref.shape)
+
+
+def analysis(trig_t, grid, sets):
     lat_dev, lon_dev, channels = grid.shape
     columns = trig_t.shape[0]
+    per_set = columns // sets
     return pl.pallas_call(
         analysis_body,
         grid=(lat_dev,),
@@ -52,8 +52,8 @@
             pl.BlockSpec((columns, lon_dev), lambda a: (0, 0)),
             pl.BlockSpec((1, lon_dev, channels), lambda a: (a, 0, 0)),
         ],
-        out_specs=pl.BlockSpec((1, columns, channels), lambda a: (a, 0, 0)),
-        out_shape=jax.ShapeDtypeStruct((lat_dev, columns, channels), jnp.bfloat16),
+        out_specs=pl.BlockSpec((sets, 1, per_set, channels), lambda a: (0, a, 0, 0)),
+        out_shape=jax.ShapeDtypeStruct((sets, lat_dev, per_set, channels), jnp.bfloat16),
         compiler_params=params(),
         cost_estimate=cost(
             2 * columns * lon_dev * lat_dev * channels,
@@ -136,15 +136,16 @@
     lax.fori_loop(0, out_ref.shape[0], step, 0, unroll=4)
 
 
-def pack(source, contrib):
+def pack(source, contrib, half):
     count = source.shape[0]
-    shape = (count,) + contrib.shape[1:]
+    blocks, cells, channels = contrib.shape
+    shape = (count, cells // 2, channels)
     return pl.pallas_call(
         pack_body,
         grid_spec=pltpu.PrefetchScalarGridSpec(
             num_scalar_prefetch=1,
             grid=(1,),
-            in_specs=[pl.BlockSpec(contrib.shape, lambda i, s: (0, 0, 0))],
+            in_specs=[pl.BlockSpec((blocks, cells // 2, channels), lambda i, s: (0, half, 0))],
             out_specs=pl.BlockSpec(shape, lambda i, s: (0, 0, 0)),
         ),
         out_shape=jax.ShapeDtypeStruct(shape, jnp.bfloat16),
@@ -186,41 +187,73 @@
     )(target, values)
 
 
-def synthesis_body(trig_ref, rows_ref, *refs):
-    deposits, out_ref = refs[:-1], refs[-1]
+def synthesis_body(trig_ref, rows_ref, first_ref, out_ref):
     sets, _, per_set, channels = rows_ref.shape
+    half = first_ref.shape[1]
     rows = rows_ref[...].reshape(sets * per_set, channels)
     wave = jnp.dot(trig_ref[...], rows, preferred_element_type=jnp.float32) * SCALE
-    wave = wave.astype(jnp.bfloat16).astype(jnp.float32).reshape(out_ref.shape[1:])
-    start = 0
-    for part in deposits:
-        stop = start + part.shape[1]
-        out_ref[0, :, start:stop] = wave[:, start:stop] + part[...]
-        start = stop
-
-
-def synthesis(trig, rows, deposits, lat_dev, blocks_per_row):
-    sets, _, per_set, channels = rows.shape
+    wave = wave.astype(jnp.bfloat16).astype(jnp.float32).reshape(out_ref.shape)
+    out_ref[:, :half] = wave[:, :half] + first_ref[...]
+    out_ref[:, half:] = wave[:, half:]
+
+
+def synthesis(trig, rows, first):
+    sets, lat_dev, per_set, channels = rows.shape
+    block_count, half, _ = first.shape
+    per_row = block_count // lat_dev
     return pl.pallas_call(
         synthesis_body,
         grid=(lat_dev,),
         in_specs=[
             pl.BlockSpec(trig.shape, lambda a: (0, 0)),
             pl.BlockSpec((sets, 1, per_set, channels), lambda a: (0, a, 0, 0)),
-        ]
-        + [
-            pl.BlockSpec((blocks_per_row,) + part.shape[1:], lambda a: (a, 0, 0))
-            for part in deposits
+            pl.BlockSpec((per_row, half, channels), lambda a: (a, 0, 0)),
         ],
-        out_specs=pl.BlockSpec((1, blocks_per_row, BS, channels), lambda a: (a, 0, 0, 0)),
-        out_shape=jax.ShapeDtypeStruct((lat_dev, blocks_per_row, BS, channels), jnp.float32),
+        out_specs=pl.BlockSpec((per_row, BS, channels), lambda a: (a, 0, 0)),
+        out_shape=jax.ShapeDtypeStruct((block_count, BS, channels), jnp.float32),
         compiler_params=params(),
         cost_estimate=cost(
             2 * trig.size * lat_dev * channels,
-            2 * (trig.size + rows.size) + 8 * lat_dev * trig.shape[0] * channels,
+            2 * (trig.size + rows.size) + 6 * lat_dev * trig.shape[0] * channels,
         ),
         name="synthesis",
-    )(trig, rows, *deposits)
+    )(trig, rows, first)
+
+
+def finish_body(target_ref, values_ref, base_ref, out_ref):
+    out_ref[...] = base_ref[...]
+
+    def step(s, carry):
+        block = target_ref[s]
+
+        @pl.when(block >= 0)
+        def _():
+            out_ref[block] += values_ref[s].astype(jnp.float32)
+
+        return carry
+
+    lax.fori_loop(0, values_ref.shape[0], step, 0, unroll=4)
+
+
+def finish(target, values, base):
+    count, half, channels = values.shape
+    block_count = base.shape[0]
+    width = channels // 2
+    spec = pl.BlockSpec((block_count, half, width), lambda i, s: (0, 1, i))
+    return pl.pallas_call(
+        finish_body,
+        grid_spec=pltpu.PrefetchScalarGridSpec(
+            num_scalar_prefetch=1,
+            grid=(channels // width,),
+            in_specs=[pl.BlockSpec((count, half, width), lambda i, s: (0, 0, i)), spec],
+            out_specs=spec,
+        ),
+        out_shape=jax.ShapeDtypeStruct(base.shape, jnp.float32),
+        input_output_aliases={2: 0},
+        compiler_params=params(),
+        cost_estimate=cost(values.size, 2 * values.size + 4 * base.size),
+        name="finish",
+    )(target, values, base)
 
 
 def shards(
@@ -243,7 +276,6 @@
     per_set = 2 * degrees // narrow_count
     blocks_per_row = lon_dev // BS
     block_count = lat_dev * blocks_per_row
-    split = BS // 2
 
     owner_band = depart_owner[:, 0]
     block_ids = jnp.arange(block_count, dtype=jnp.int32)
@@ -254,20 +286,13 @@
     send_slot = owner_band * capacity + slot_rank
     pick_slot = jnp.arange(wide_count * capacity, dtype=jnp.int32)[:, None] == send_slot[None, :]
     source = jnp.max(jnp.where(pick_slot, block_ids[None, :], 0), axis=1)
-    slot_target = jnp.max(jnp.where(pick_slot, depart_block[None, :], -1), axis=1).reshape(
-        wide_count, capacity
-    )
-    recv_targets = lax.all_to_all(
-        slot_target, "wide", split_axis=0, concat_axis=0, tiled=True
-    ).reshape(-1)
+    tables = lax.all_gather(jnp.stack([owner_band, depart_block]), "wide", axis=0, tiled=False)
     blocks = grid_adjoint_fields.reshape(block_count, BS, channels)
     contrib = jnp.einsum(
         "bai,bac->bic", interp_weights, blocks, preferred_element_type=jnp.float32
     ).astype(jnp.bfloat16)
-    packed = [
-        pack(source, contrib[:, :split]).reshape(wide_count, capacity, split, channels),
-        pack(source, contrib[:, split:]).reshape(wide_count, capacity, BS - split, channels),
-    ]
+    def packed(source, half):
+        return pack(source, contrib, half).reshape(wide_count, capacity, BS // 2, channels)
 
     def exchange(values):
         return lax.all_to_all(values, "wide", split_axis=0, concat_axis=0, tiled=True)
@@ -279,15 +304,16 @@
     order = wavenumber.transpose(1, 0, 2).reshape(-1)
     trig = trig_tables(narrow_index * lon_dev, lon_dev, order)
 
-    first_recv = exchange(packed[0])
-    partial = analysis(trig.T, grid_adjoint_fields)
-    summed = lax.psum_scatter(
-        partial.reshape(lat_dev, narrow_count, per_set, channels),
-        "narrow",
-        scatter_dimension=1,
-        tiled=False,
-    )
-    summed, first_recv = lax.optimization_barrier((summed, first_recv))
+    first_recv = exchange(packed(source, 0))
+    partial = analysis(trig.T, grid_adjoint_fields, narrow_count)
+    partial, tables = lax.optimization_barrier((partial, tables))
+    mine = tables[:, 0] == wide_index
+    rank = jnp.sum((mine[:, None, :] & earlier[None]).astype(jnp.int32), axis=2)
+    rank = jnp.where(mine, rank, -1)
+    arriving = rank[:, None, :] == jnp.arange(capacity, dtype=jnp.int32)[None, :, None]
+    recv_targets = jnp.max(jnp.where(arriving, tables[:, 1][:, None, :], -1), axis=2).reshape(-1)
+    summed = lax.psum_scatter(partial, "narrow", scatter_dimension=0, tiled=False)
+    summed, first_recv, source = lax.optimization_barrier((summed, first_recv, source))
     fourier = exchange(
         summed.reshape(lat_dev, wide_count, 2 * slot_count, channels).transpose(1, 2, 0, 3)
     )
@@ -302,16 +328,16 @@
         damping,
     )
     synth = exchange(synth)
-    synth, second = lax.optimization_barrier((synth, packed[1]))
+    synth, second = lax.optimization_barrier((synth, packed(source, 1)))
     second_recv = exchange(second)
     rows = lax.all_gather(
         synth.reshape(per_set, lat_dev, channels).transpose(1, 0, 2), "narrow", axis=0, tiled=False
     )
-    deposits = [
-        deposit(recv_targets, recv.reshape(wide_count * capacity, -1, channels), block_count)
-        for recv in (first_recv, second_recv)
-    ]
-    out = synthesis(trig, rows, deposits, lat_dev, blocks_per_row)
+    first = deposit(
+        recv_targets, first_recv.reshape(wide_count * capacity, -1, channels), block_count
+    )
+    base = synthesis(trig, rows, first)
+    out = finish(recv_targets, second_recv.reshape(wide_count * capacity, -1, channels), base)
     return out.reshape(lat_dev, lon_dev, channels)
 
 

time: 458 us -> 448 us (0.978)
  waiting for transfers between devices: 192 us -> 178 us
  local copies, waits for them, and re-layouts: 28.3 us -> 16.5 us
  blocking collectives: 133 us -> 142 us
    all_to_all x3, waiting for transfers between devices: 192 us -> 136 us  [exchange(): lax.all_to_all(values, 'wide', split_axis=0, concat_axis=0, tiled=True)]
    all_gather x1, waiting for transfers between devices: 0.01 us -> 41.8 us  [shards(): lax.all_gather(synth.reshape(per_set, lat_dev, channels).transpose(1, 0,...]
    all_gather x0 -> x1, blocking collectives: none -> 27.8 us  [shards(): lax.all_gather(jnp.stack([owner_band, depart_block]), 'wide', axis=0, til...]
    pallas_call x0 -> x1, Pallas kernels: none -> 12.2 us  [finish(): pl.pallas_call(finish_body, grid_spec=pltpu.PrefetchScalarGridSpec(num_sc...]
    reshape x2 -> x1, local copies, waits for them, and re-layouts: 11.5 us -> 0.08 us  [shards(): jnp.max(jnp.where(arriving, tables[:, 1][:, None, :], -1), axis=2)]
    all_to_all x1 -> x0, blocking collectives: 9.89 us -> none  [shards(): lax.all_to_all(slot_target, 'wide', split_axis=0, concat_axis=0, tiled=True)]
    all_to_all x1, blocking collectives: 123 us -> 114 us  [exchange(): lax.all_to_all(values, 'wide', split_axis=0, concat_axis=0, tiled=True)]
    pallas_call x2 -> x1, Pallas kernels: 14.7 us -> 8.03 us  [deposit(): pl.pallas_call(deposit_body, grid_spec=pltpu.PrefetchScalarGridSpec(num_s...]
  transfers between devices with their start and end apart: 5 -> 5, of which waited for: 3 -> 4; matrix products, arithmetic and copies ran while one was open for 2% -> 3% of each run, Pallas kernels for 5% -> 6%
where the time goes in v2:
time: 448 us; the launch traced here: 447 us
  waiting for transfers between devices  178 us (40%)
  blocking collectives  142 us (32%)
  Pallas kernels  71.9 us (16%)
  local copies, waits for them, and re-layouts  16.5 us (4%)
  between operations  13.7 us (3%)
  starting transfers between devices  12.8 us (3%)
  matrix products  7.69 us (2%)
  other arithmetic  4.72 us (1%)
    all_to_all x3, waiting for transfers between devices, exchange(): lax.all_to_all(values, 'wide', split_axis=0, concat_axis=0, tiled=True)  136 us
    all_to_all x1, blocking collectives, exchange(): lax.all_to_all(values, 'wide', split_axis=0, concat_axis=0, tiled=True)  114 us
    all_gather x1, waiting for transfers between devices, shards(): lax.all_gather(synth.reshape(per_set, lat_dev, channels).transpose(1, 0,...  41.8 us
    all_gather x1, blocking collectives, shards(): lax.all_gather(jnp.stack([owner_band, depart_block]), 'wide', axis=0, til...  27.8 us
    pallas_call x1, Pallas kernels, modes(): pl.pallas_call(modes_body, grid_spec=pltpu.PrefetchScalarGridSpec(num_sca...  20.1 us
    pallas_call x1, Pallas kernels, synthesis(): pl.pallas_call(synthesis_body, grid=(lat_dev,), in_specs=[pl.BlockSpec(tr...  13.2 us
    all_to_all x3, starting transfers between devices, exchange(): lax.all_to_all(values, 'wide', split_axis=0, concat_axis=0, tiled=True)  12.8 us
    pallas_call x1, Pallas kernels, finish(): pl.pallas_call(finish_body, grid_spec=pltpu.PrefetchScalarGridSpec(num_sc...  12.2 us
  transfers between devices with their start and end apart: 5, of which 4 were waited for; matrix products, arithmetic and copies ran while one was open for 3% of the time, Pallas kernels for 6%

profile of v2, /device:TPU:0, one launch (start us, length us, event | category | flops | bytes accessed | tf_op | source)
XLA Modules:
  0.0 446.7 jit_solution(1339225037049253098)
XLA Ops:
  7.3 27.8 %all-gather.2 = s32[8,2,160]{2,1,0:T(2,128)S(1)} all-gather(s32[1,2,160]{2,1,0:T(2,128)S(1)} %add_bitcast_fusion), channel_id=2, replica_groups=mesh['wide'=8,'narrow'=4] {'wide'}, dimensions={0}, use_global_device_ids=true | all-gather | bytes 11520 | tf_op jit(solution)/shard_map/all_gather | solution.py:289
  38.5 11.5 %analysis.1 = bf16[4,8,256,512]{3,2,1,0:T(8,128)(2,1)} custom-call(bf16[1024,640]{1,0:T(8,128)(2,1)S(1)} %copy.27.trig_ref, bf16[8,640,512]{2,1,0:T(8,128)(2,1)} %grid_ref.1), custom_call_target="tpu_custom_call" | custom-call | flops 5368709120 | bytes 14942208 | tf_op jit(solution)/shard_map/analysis/pallas_call | solution.py:48
  51.0 1.5 copy.29
  52.9 7.7 %convolution_convert_fusion.contrib_ref = bf16[160,32,512]{2,1,0:T(8,128)(2,1)} fusion(bf16[160,32,32]{1,2,0:T(8,128)(2,1)S(1)} %copy.29, bf16[160,32,512]{2,1,0:T(8,128)(2,1)} %bitcast.46), kind=kOutput, calls=%fused_computation | convolution fusion | flops 170393600 | bytes 10813440 | tf_op jit(solution)/shard_map/bai,bac->bic/dot_general | solution.py:291
  60.6 3.6 pack.2
  64.2 114.1 %all_to_all.20 = bf16[8,40,16,512]{3,2,1,0:T(8,128)(2,1)} all-to-all(bf16[8,40,16,512]{3,2,1,0:T(8,128)(2,1)S(1)} %bitcast.39), channel_id=1, replica_groups=mesh['wide'=8,'narrow'=4] {'wide'}, dimensions={0} | all-to-all | bytes 10485760 | tf_op jit(solution)/shard_map/all_to_all | solution.py:298
  178.3 4.1 copy.30
  182.3 4.5 %all-to-all-start.1 = ((bf16[8,32,8,512]{3,2,1,0:T(8,128)(2,1)}), bf16[8,32,8,512]{3,2,1,0:T(8,128)(2,1)}, u32[]{:S(2)}, u32[]{:S(2)}) async-start(bf16[8,32,8,512]{3,2,1,0:T(8,128)(2,1)} %bitcast.15), calls=%async_computation.2 | async-start | bytes 4194304 | tf_op jit(solution)/shard_map/all_to_all | solution.py:298
  186.9 1.3 convert_element_type.36.back_ref
  188.5 44.3 %all-to-all-done.1.fourier_ref = bf16[8,32,8,512]{3,2,1,0:T(8,128)(2,1)} async-done(((bf16[8,32,8,512]{3,2,1,0:T(8,128)(2,1)}), bf16[8,32,8,512]{3,2,1,0:T(8,128)(2,1)}, u32[]{:S(2)}, u32[]{:S(2)}) %all-to-all-start.1) | async-done | bytes 2097184 | tf_op jit(solution)/shard_map/all_to_all | solution.py:298
  232.8 1.2 copy-done.2
  234.0 20.1 %modes.1 = bf16[8,32,8,512]{3,2,1,0:T(8,128)(2,1)} custom-call(s32[16]{0:T(128)S(1)} %dynamic-slice_bitcast_fusion.wave_ref, bf16[16,64,512]{2,1,0:T(8,128)(2,1)S(1)} %copy-done.2, bf16[8,32,8,512]{3,2,1,0:T(8,128)(2,1)} %all-to-all-done.1.fourier_ref, bf16[512,512]{1,0:T(8,128)(2,1)S(1)} %convert_element_type.35.proj_ref, ...), custom_call_target="tpu_custom_call" | custom-call | flops 4294967296 | bytes 7340032 | tf_op jit(solution)/shard_map/modes/pallas_call | solution.py:107
  254.1 3.6 all-to-all-start.2
  257.8 3.1 pack.3
  260.9 2.3 copy-done
  263.2 42.8 %all-to-all-done.2 = bf16[8,32,8,512]{3,2,1,0:T(8,128)(2,1)S(1)} async-done(((bf16[8,32,8,512]{3,2,1,0:T(8,128)(2,1)}), bf16[8,32,8,512]{3,2,1,0:T(8,128)(2,1)S(1)}, u32[]{:S(2)}, u32[]{:S(2)}) %all-to-all-start.2) | async-done | bytes 2097184 | tf_op jit(solution)/shard_map/all_to_all | solution.py:298
  306.0 2.0 copy.35
  308.0 4.7 %all-to-all-start.3 = ((bf16[8,40,16,512]{3,2,1,0:T(8,128)(2,1)}), bf16[8,40,16,512]{3,2,1,0:T(8,128)(2,1)}, u32[]{:S(2)}, u32[]{:S(2)}) async-start(bf16[8,40,16,512]{3,2,1,0:T(8,128)(2,1)} %bitcast.38), calls=%async_computation.4 | async-start | bytes 10485760 | tf_op jit(solution)/shard_map/all_to_all | solution.py:298
  313.5 8.0 %deposit.1.first_ref = f32[160,16,512]{2,1,0:T(8,128)S(1)} custom-call(s32[320]{0:T(512)S(1)} %reshape.92.target_ref, bf16[320,16,512]{2,1,0:T(8,128)(2,1)} %bitcast.42), custom_call_target="tpu_custom_call" | custom-call | flops 2621440 | bytes 10485760 | tf_op jit(solution)/shard_map/deposit/pallas_call | solution.py:175
  321.5 2.4 copy-done.1
  323.9 41.8 %all-gather.5.cloned.1.call-done = bf16[32,256,512]{2,1,0:T(8,128)(2,1)} async-done(((bf16[8,256,512]{2,1,0:T(8,128)(2,1)}), bf16[32,256,512]{2,1,0:T(8,128)(2,1)}) %all-gather.5.cloned.1.call-update) | async-done | bytes 8388624 | tf_op jit(solution)/shard_map/all_gather | solution.py:333
  365.7 13.2 %synthesis.1.base_ref = f32[160,32,512]{2,1,0:T(8,128)} custom-call(bf16[640,1024]{1,0:T(8,128)(2,1)S(1)} %bitcast.41, bf16[4,8,256,512]{3,2,1,0:T(8,128)(2,1)} %bitcast.43, f32[160,16,512]{2,1,0:T(8,128)} %copy-done.1), custom_call_target="tpu_custom_call" | custom-call | flops 5368709120 | bytes 25427968 | tf_op jit(solution)/shard_map/synthesis/pallas_call | solution.py:204
  378.9 48.7 %all-to-all-done.3 = bf16[8,40,16,512]{3,2,1,0:T(8,128)(2,1)} async-done(((bf16[8,40,16,512]{3,2,1,0:T(8,128)(2,1)}), bf16[8,40,16,512]{3,2,1,0:T(8,128)(2,1)}, u32[]{:S(2)}, u32[]{:S(2)}) %all-to-all-start.3) | async-done | bytes 5242912 | tf_op jit(solution)/shard_map/all_to_all | solution.py:298
  427.6 12.2 %finish.1 = f32[160,32,512]{2,1,0:T(8,128)} custom-call(s32[320]{0:T(512)S(1)} %reshape.92.target_ref, bf16[320,16,512]{2,1,0:T(8,128)(2,1)} %bitcast.17.values_ref, f32[160,32,512]{2,1,0:T(8,128)} %synthesis.1.base_ref), custom_call_target="tpu_custom_call", output_to_operand_aliasing={{}: (2, {})} | custom-call | flops 2621440 | bytes 15728640 | tf_op jit(solution)/shard_map/finish/pallas_call | solution.py:243
  (43 shorter events, 6.5 us)
Async XLA Ops:
  6.5 171.7 %reduce-scatter.2.cloned.1.call-start = ((), (), s32[]{:S(2)}) async-start(), calls=%async_computation.5 | async-start | bytes 10485760 | tf_op jit(solution)/shard_map/reduce_scatter | solution.py:315
  50.0 1.0 copy-start.4
  50.0 2.5 copy-start.5
  182.3 4.5 %copy-start.3 = (f32[512,512]{1,0:T(8,128)S(1)}, f32[512,512]{1,0:T(8,128)}, u32[]{:S(2)}) copy-start(f32[512,512]{1,0:T(8,128)} %param.15) | copy-start | bytes 3145732
  182.3 50.4 %all-to-all-start.1 = ((bf16[8,32,8,512]{3,2,1,0:T(8,128)(2,1)}), bf16[8,32,8,512]{3,2,1,0:T(8,128)(2,1)}, u32[]{:S(2)}, u32[]{:S(2)}) async-start(bf16[8,32,8,512]{3,2,1,0:T(8,128)(2,1)} %bitcast.15), calls=%async_computation.2 | async-start | bytes 4194304 | tf_op jit(solution)/shard_map/all_to_all | solution.py:298
  186.8 1.4 copy-start.6
  232.8 1.2 copy-start.2
  254.1 51.8 %all-to-all-start.2 = ((bf16[8,32,8,512]{3,2,1,0:T(8,128)(2,1)}), bf16[8,32,8,512]{3,2,1,0:T(8,128)(2,1)S(1)}, u32[]{:S(2)}, u32[]{:S(2)}) async-start(bf16[8,32,8,512]{3,2,1,0:T(8,128)(2,1)} %modes.1), calls=%async_computation.3 | async-start | bytes 4194304 | tf_op jit(solution)/shard_map/all_to_all | solution.py:298
  257.8 107.9 %all-gather.5.cloned.1.call-start = ((), (), s32[]{:S(2)}) async-start(), calls=%async_computation.6 | async-start | bytes 10485760 | tf_op jit(solution)/shard_map/all_gather | solution.py:333
  260.9 2.3 copy-start
  308.0 119.6 %all-to-all-start.3 = ((bf16[8,40,16,512]{3,2,1,0:T(8,128)(2,1)}), bf16[8,40,16,512]{3,2,1,0:T(8,128)(2,1)}, u32[]{:S(2)}, u32[]{:S(2)}) async-start(bf16[8,40,16,512]{3,2,1,0:T(8,128)(2,1)} %bitcast.38), calls=%async_computation.4 | async-start | bytes 10485760 | tf_op jit(solution)/shard_map/all_to_all | solution.py:298
  321.5 2.4 copy-start.1
Sparse Core Ops, SparseCore 0:
  50.1 71.1 reduce-scatter.1
  308.2 57.5 all-gather.4

commit v3 on v2

--- a/solution.py
+++ b/solution.py
@@ -64,25 +64,28 @@
 
 
 def modes_body(wave_ref, legendre_ref, fourier_ref, proj_ref, back_ref, damping_ref, out_ref):
-    slot = pl.program_id(0)
-    bands, parts, lat_dev, channels = fourier_ref.shape
+    bands, count, lat_dev, channels = fourier_ref.shape
     lats = bands * lat_dev
-    degrees = legendre_ref.shape[2]
+    slots, _, degrees = legendre_ref.shape
+    first_slot = pl.program_id(0) * slots
     degree = lax.broadcasted_iota(jnp.int32, (lats, degrees), 1)
-    masked = jnp.where(
-        degree >= wave_ref[slot], legendre_ref[0].astype(jnp.float32), 0.0
-    ).astype(jnp.bfloat16)
     fourier = fourier_ref[...].astype(jnp.float32)
     rows = jnp.concatenate(
-        [fourier[:, p].reshape(lats, channels) for p in range(parts)], axis=0
+        [fourier[:, q].reshape(lats, channels) for q in range(count)], axis=0
     ).astype(jnp.bfloat16)
     projected = jnp.dot(rows, proj_ref[...], preferred_element_type=jnp.float32) * SCALE
     projected = projected.astype(jnp.bfloat16)
     sums = []
-    for p in range(parts):
+    for q in range(count):
+        if q % 2 == 0:
+            masked = jnp.where(
+                degree >= wave_ref[first_slot + q // 2],
+                legendre_ref[q // 2].astype(jnp.float32),
+                0.0,
+            ).astype(jnp.bfloat16)
         modal = lax.dot_general(
             masked,
-            projected[p * lats : (p + 1) * lats],
+            projected[q * lats : (q + 1) * lats],
             (((0,), (0,)), ((), ())),
             preferred_element_type=jnp.float32,
         )
@@ -93,24 +96,25 @@
         back_ref[...],
         preferred_element_type=jnp.float32,
     )
-    for p in range(parts):
-        out_ref[:, p] = (
-            back[p * lats : (p + 1) * lats].reshape(bands, lat_dev, channels).astype(jnp.bfloat16)
+    for q in range(count):
+        out_ref[:, q] = (
+            back[q * lats : (q + 1) * lats].reshape(bands, lat_dev, channels).astype(jnp.bfloat16)
         )
 
 
 def modes(wavenumber, legendre, fourier, proj, back, damping):
     slots, lats, degrees = legendre.shape
     bands, _, lat_dev, channels = fourier.shape
-    spec = pl.BlockSpec((bands, 2, lat_dev, channels), lambda j, w: (0, j, 0, 0))
+    group = math.gcd(slots, 4)
+    spec = pl.BlockSpec((bands, 2 * group, lat_dev, channels), lambda j, w: (0, j, 0, 0))
     whole = lambda j, w: (0, 0)
     return pl.pallas_call(
         modes_body,
         grid_spec=pltpu.PrefetchScalarGridSpec(
             num_scalar_prefetch=1,
-            grid=(slots,),
+            grid=(slots // group,),
             in_specs=[
-                pl.BlockSpec((1, lats, degrees), lambda j, w: (j, 0, 0)),
+                pl.BlockSpec((group, lats, degrees), lambda j, w: (j, 0, 0)),
                 spec,
                 pl.BlockSpec(proj.shape, whole),
                 pl.BlockSpec(back.shape, whole),
@@ -128,15 +132,22 @@
     )(wavenumber, legendre, fourier, proj, back, damping)
 
 
-def pack_body(source_ref, contrib_ref, out_ref):
+def pack_body(source_ref, contrib_ref, *refs):
+    out_ref = refs[-1]
+
     def step(s, carry):
         out_ref[s] = contrib_ref[source_ref[s]]
         return carry
 
     lax.fori_loop(0, out_ref.shape[0], step, 0, unroll=4)
-
-
-def pack(source, contrib, half):
+    if len(refs) == 2:
+        table_ref = refs[0]
+        per_owner = out_ref.shape[0] // table_ref.shape[0]
+        for owner in range(table_ref.shape[0]):
+            out_ref[(owner + 1) * per_owner - 1] = table_ref[owner]
+
+
+def pack(source, contrib, half, *table):
     count = source.shape[0]
     blocks, cells, channels = contrib.shape
     shape = (count, cells // 2, channels)
@@ -145,14 +156,15 @@
         grid_spec=pltpu.PrefetchScalarGridSpec(
             num_scalar_prefetch=1,
             grid=(1,),
-            in_specs=[pl.BlockSpec((blocks, cells // 2, channels), lambda i, s: (0, half, 0))],
+            in_specs=[pl.BlockSpec((blocks, cells // 2, channels), lambda i, s: (0, half, 0))]
+            + [pl.BlockSpec(t.shape, lambda i, s: (0, 0, 0)) for t in table],
             out_specs=pl.BlockSpec(shape, lambda i, s: (0, 0, 0)),
         ),
         out_shape=jax.ShapeDtypeStruct(shape, jnp.bfloat16),
         compiler_params=params(),
         cost_estimate=cost(math.prod(shape), 4 * math.prod(shape)),
         name="pack",
-    )(source, contrib)
+    )(source, contrib, *table)
 
 
 def deposit_body(target_ref, values_ref, out_ref):
@@ -286,14 +298,16 @@
     send_slot = owner_band * capacity + slot_rank
     pick_slot = jnp.arange(wide_count * capacity, dtype=jnp.int32)[:, None] == send_slot[None, :]
     source = jnp.max(jnp.where(pick_slot, block_ids[None, :], 0), axis=1)
-    tables = lax.all_gather(jnp.stack([owner_band, depart_block]), "wide", axis=0, tiled=False)
+    slot_target = jnp.max(jnp.where(pick_slot, depart_block[None, :], -1), axis=1).reshape(
+        wide_count, capacity
+    )
+    table = jnp.pad(slot_target.astype(jnp.bfloat16), ((0, 0), (0, channels - capacity)))
+    table = jnp.broadcast_to(table[:, None, :], (wide_count, BS // 2, channels))
+    first_source = jnp.pad(source.reshape(wide_count, capacity), ((0, 0), (0, 1))).reshape(-1)
     blocks = grid_adjoint_fields.reshape(block_count, BS, channels)
     contrib = jnp.einsum(
         "bai,bac->bic", interp_weights, blocks, preferred_element_type=jnp.float32
     ).astype(jnp.bfloat16)
-    def packed(source, half):
-        return pack(source, contrib, half).reshape(wide_count, capacity, BS // 2, channels)
-
     def exchange(values):
         return lax.all_to_all(values, "wide", split_axis=0, concat_axis=0, tiled=True)
 
@@ -304,14 +318,10 @@
     order = wavenumber.transpose(1, 0, 2).reshape(-1)
     trig = trig_tables(narrow_index * lon_dev, lon_dev, order)
 
-    first_recv = exchange(packed(source, 0))
+    first_recv = exchange(
+        pack(first_source, contrib, 0, table).reshape(wide_count, capacity + 1, BS // 2, channels)
+    )
     partial = analysis(trig.T, grid_adjoint_fields, narrow_count)
-    partial, tables = lax.optimization_barrier((partial, tables))
-    mine = tables[:, 0] == wide_index
-    rank = jnp.sum((mine[:, None, :] & earlier[None]).astype(jnp.int32), axis=2)
-    rank = jnp.where(mine, rank, -1)
-    arriving = rank[:, None, :] == jnp.arange(capacity, dtype=jnp.int32)[None, :, None]
-    recv_targets = jnp.max(jnp.where(arriving, tables[:, 1][:, None, :], -1), axis=2).reshape(-1)
     summed = lax.psum_scatter(partial, "narrow", scatter_dimension=0, tiled=False)
     summed, first_recv, source = lax.optimization_barrier((summed, first_recv, source))
     fourier = exchange(
@@ -328,13 +338,16 @@
         damping,
     )
     synth = exchange(synth)
-    synth, second = lax.optimization_barrier((synth, packed(source, 1)))
-    second_recv = exchange(second)
+    synth, second = lax.optimization_barrier((synth, pack(source, contrib, 1)))
+    second_recv = exchange(second.reshape(wide_count, capacity, BS // 2, channels))
     rows = lax.all_gather(
         synth.reshape(per_set, lat_dev, channels).transpose(1, 0, 2), "narrow", axis=0, tiled=False
     )
+    recv_targets = first_recv[:, capacity, 0, :capacity].astype(jnp.int32)
+    first_targets = jnp.pad(recv_targets, ((0, 0), (0, 1)), constant_values=-1).reshape(-1)
+    recv_targets = recv_targets.reshape(-1)
     first = deposit(
-        recv_targets, first_recv.reshape(wide_count * capacity, -1, channels), block_count
+        first_targets, first_recv.reshape(first_targets.shape[0], -1, channels), block_count
     )
     base = synthesis(trig, rows, first)
     out = finish(recv_targets, second_recv.reshape(wide_count * capacity, -1, channels), base)

time: 448 us -> 425 us (0.949)
  blocking collectives: 142 us -> 126 us
  local copies, waits for them, and re-layouts: 16.5 us -> 27 us
  waiting for transfers between devices: 178 us -> 171 us
  Pallas kernels: 71.9 us -> 66.3 us
    all_gather x1 -> x0, blocking collectives: 27.8 us -> none  [shards(): lax.all_gather(jnp.stack([owner_band, depart_block]), 'wide', axis=0, til...]
    all_to_all x1, blocking collectives: 114 us -> 126 us  [exchange(): lax.all_to_all(values, 'wide', split_axis=0, concat_axis=0, tiled=True)]
    optimization_barrier x1 -> x2, local copies, waits for them, and re-layouts: 4.07 us -> 13.5 us  [shards(): lax.optimization_barrier((summed, first_recv, source))]
    all_gather x1, waiting for transfers between devices: 41.8 us -> 33.4 us  [shards(): lax.all_gather(synth.reshape(per_set, lat_dev, channels).transpose(1, 0,...]
    pallas_call x1, Pallas kernels: 20.1 us -> 14.9 us  [modes(): pl.pallas_call(modes_body, grid_spec=pltpu.PrefetchScalarGridSpec(num_sca...]
    unnamed x15 -> x19, local copies, waits for them, and re-layouts: 8.39 us -> 9.13 us
  transfers between devices with their start and end apart: 5 -> 5, of which waited for: 4 -> 4; matrix products, arithmetic and copies ran while one was open for 3% -> 4% of each run, Pallas kernels for 6% -> 7%
where the time goes in v3:
time: 425 us; the launch traced here: 424 us
  waiting for transfers between devices  171 us (40%)
  blocking collectives  126 us (30%)
  Pallas kernels  66.3 us (16%)
  local copies, waits for them, and re-layouts  27 us (6%)
  between operations  13.7 us (3%)
  starting transfers between devices  13 us (3%)
    all_to_all x3, waiting for transfers between devices, exchange(): lax.all_to_all(values, 'wide', split_axis=0, concat_axis=0, tiled=True)  137 us
    all_to_all x1, blocking collectives, exchange(): lax.all_to_all(values, 'wide', split_axis=0, concat_axis=0, tiled=True)  126 us
    all_gather x1, waiting for transfers between devices, shards(): lax.all_gather(synth.reshape(per_set, lat_dev, channels).transpose(1, 0,...  33.4 us
    pallas_call x1, Pallas kernels, modes(): pl.pallas_call(modes_body, grid_spec=pltpu.PrefetchScalarGridSpec(num_sca...  14.9 us
    optimization_barrier x2, local copies, waits for them, and re-layouts, shards(): lax.optimization_barrier((summed, first_recv, source))  13.5 us
    pallas_call x1, Pallas kernels, synthesis(): pl.pallas_call(synthesis_body, grid=(lat_dev,), in_specs=[pl.BlockSpec(tr...  13.2 us
    all_to_all x3, starting transfers between devices, exchange(): lax.all_to_all(values, 'wide', split_axis=0, concat_axis=0, tiled=True)  12.9 us
    pallas_call x1, Pallas kernels, finish(): pl.pallas_call(finish_body, grid_spec=pltpu.PrefetchScalarGridSpec(num_sc...  12.1 us
  transfers between devices with their start and end apart: 5, of which 4 were waited for; matrix products, arithmetic and copies ran while one was open for 4% of the time, Pallas kernels for 7%

profile of v3, /device:TPU:0, one launch (start us, length us, event | category | flops | bytes accessed | tf_op | source)
XLA Modules:
  0.0 423.9 jit_solution(6968140404650456644)
XLA Ops:
  10.0 11.5 %analysis.1 = bf16[4,8,256,512]{3,2,1,0:T(8,128)(2,1)} custom-call(bf16[1024,640]{1,0:T(8,128)(2,1)S(1)} %copy.29.trig_ref, bf16[8,640,512]{2,1,0:T(8,128)(2,1)} %grid_ref.1), custom_call_target="tpu_custom_call" | custom-call | flops 5368709120 | bytes 14942208 | tf_op jit(solution)/shard_map/analysis/pallas_call | solution.py:48
  22.7 1.5 copy.30
  24.3 4.0 convolution_convert_fusion.contrib_ref
  28.4 4.0 pack.2
  33.5 126.0 %all_to_all.20 = bf16[8,41,16,512]{3,2,1,0:T(8,128)(2,1)} all-to-all(bf16[8,41,16,512]{3,2,1,0:T(8,128)(2,1)} %bitcast.34), channel_id=1, replica_groups=mesh['wide'=8,'narrow'=4] {'wide'}, dimensions={0} | all-to-all | bytes 10747904 | tf_op jit(solution)/shard_map/all_to_all | solution.py:312
  159.5 4.1 copy.32
  163.6 4.5 %all-to-all-start.1 = ((bf16[8,32,8,512]{3,2,1,0:T(8,128)(2,1)}), bf16[8,32,8,512]{3,2,1,0:T(8,128)(2,1)}, u32[]{:S(2)}, u32[]{:S(2)}) async-start(bf16[8,32,8,512]{3,2,1,0:T(8,128)(2,1)} %bitcast.9), calls=%async_computation.2 | async-start | bytes 4194304 | tf_op jit(solution)/shard_map/all_to_all | solution.py:312
  168.1 1.3 convert_element_type.54.back_ref
  169.7 45.3 %all-to-all-done.1.fourier_ref = bf16[8,32,8,512]{3,2,1,0:T(8,128)(2,1)} async-done(((bf16[8,32,8,512]{3,2,1,0:T(8,128)(2,1)}), bf16[8,32,8,512]{3,2,1,0:T(8,128)(2,1)}, u32[]{:S(2)}, u32[]{:S(2)}) %all-to-all-start.1) | async-done | bytes 2097184 | tf_op jit(solution)/shard_map/all_to_all | solution.py:312
  215.0 1.2 copy-done.3
  216.3 14.9 %modes.1 = bf16[8,32,8,512]{3,2,1,0:T(8,128)(2,1)} custom-call(s32[16]{0:T(128)S(1)} %dynamic-slice_bitcast_fusion.wave_ref, bf16[16,64,512]{2,1,0:T(8,128)(2,1)S(1)} %copy-done.3, bf16[8,32,8,512]{3,2,1,0:T(8,128)(2,1)} %all-to-all-done.1.fourier_ref, bf16[512,512]{1,0:T(8,128)(2,1)S(1)} %convert_element_type.53.proj_ref, ...), custom_call_target="tpu_custom_call" | custom-call | flops 4294967296 | bytes 7340032 | tf_op jit(solution)/shard_map/modes/pallas_call | solution.py:111
  231.2 3.6 all-to-all-start.2
  234.8 3.1 pack.3
  237.9 2.3 copy-done.1
  240.2 43.0 %all-to-all-done.2 = bf16[8,32,8,512]{3,2,1,0:T(8,128)(2,1)S(1)} async-done(((bf16[8,32,8,512]{3,2,1,0:T(8,128)(2,1)}), bf16[8,32,8,512]{3,2,1,0:T(8,128)(2,1)S(1)}, u32[]{:S(2)}, u32[]{:S(2)}) %all-to-all-start.2) | async-done | bytes 2097184 | tf_op jit(solution)/shard_map/all_to_all | solution.py:312
  283.2 2.0 copy.35
  285.3 4.9 %all-to-all-start.3 = ((bf16[8,40,16,512]{3,2,1,0:T(8,128)(2,1)}), bf16[8,40,16,512]{3,2,1,0:T(8,128)(2,1)}, u32[]{:S(2)}, u32[]{:S(2)}) async-start(bf16[8,40,16,512]{3,2,1,0:T(8,128)(2,1)} %bitcast.30), calls=%async_computation.4 | async-start | bytes 10485760 | tf_op jit(solution)/shard_map/all_to_all | solution.py:312
  290.1 9.5 %copy.31 = bf16[8,41,16,512]{3,0,2,1:T(8,128)(2,1)S(1)} copy(bf16[8,41,16,512]{3,2,1,0:T(8,128)(2,1)} %all_to_all.20) | data formatting | bytes 10747904 | tf_op jit(solution)/shard_map/optimization_barrier | solution.py:326
  299.8 7.3 %deposit.1.first_ref = f32[160,16,512]{2,1,0:T(8,128)S(1)} custom-call(s32[328]{0:T(512)S(1)} %reshape.111.target_ref, bf16[328,16,512]{2,1,0:T(8,128)(2,1)} %bitcast.33), custom_call_target="tpu_custom_call" | custom-call | flops 2686976 | bytes 10616832 | tf_op jit(solution)/shard_map/deposit/pallas_call | solution.py:187
  307.1 2.4 copy-done.2
  309.5 33.4 %all-gather.3.cloned.1.call-done = bf16[32,256,512]{2,1,0:T(8,128)(2,1)} async-done(((bf16[8,256,512]{2,1,0:T(8,128)(2,1)}), bf16[32,256,512]{2,1,0:T(8,128)(2,1)}) %all-gather.3.cloned.1.call-update) | async-done | bytes 8388624 | tf_op jit(solution)/shard_map/all_gather | solution.py:343
  342.9 13.2 %synthesis.1.base_ref = f32[160,32,512]{2,1,0:T(8,128)} custom-call(bf16[640,1024]{1,0:T(8,128)(2,1)S(1)} %bitcast.32, bf16[4,8,256,512]{3,2,1,0:T(8,128)(2,1)} %bitcast.35, f32[160,16,512]{2,1,0:T(8,128)} %copy-done.2), custom_call_target="tpu_custom_call" | custom-call | flops 5368709120 | bytes 25427968 | tf_op jit(solution)/shard_map/synthesis/pallas_call | solution.py:216
  356.1 48.8 %all-to-all-done.3 = bf16[8,40,16,512]{3,2,1,0:T(8,128)(2,1)} async-done(((bf16[8,40,16,512]{3,2,1,0:T(8,128)(2,1)}), bf16[8,40,16,512]{3,2,1,0:T(8,128)(2,1)}, u32[]{:S(2)}, u32[]{:S(2)}) %all-to-all-start.3) | async-done | bytes 5242912 | tf_op jit(solution)/shard_map/all_to_all | solution.py:312
  404.9 12.1 %finish.1 = f32[160,32,512]{2,1,0:T(8,128)} custom-call(s32[320]{0:T(512)S(1)} %reshape.109.target_ref, bf16[320,16,512]{2,1,0:T(8,128)(2,1)} %bitcast.11.values_ref, f32[160,32,512]{2,1,0:T(8,128)} %synthesis.1.base_ref), custom_call_target="tpu_custom_call", output_to_operand_aliasing={{}: (2, {})} | custom-call | flops 2621440 | bytes 15728640 | tf_op jit(solution)/shard_map/finish/pallas_call | solution.py:255
  (49 shorter events, 6.3 us)
Async XLA Ops:
  6.5 152.9 %reduce-scatter.2.cloned.1.call-start = ((), (), s32[]{:S(2)}) async-start(), calls=%async_computation.5 | async-start | bytes 10485760 | tf_op jit(solution)/shard_map/reduce_scatter | solution.py:325
  21.5 0.7 copy-start.6
  21.5 0.9 copy-start.8
  21.5 1.2 copy-start.5
  28.4 5.1 %copy-start = (bf16[160,32,512]{2,1,0:T(8,128)(2,1)}, bf16[160,32,512]{2,1,0:T(8,128)(2,1)S(1)}, u32[]{:S(2)}) copy-start(bf16[160,32,512]{2,1,0:T(8,128)(2,1)S(1)} %convolution_convert_fusion.contrib_ref) | copy-start | bytes 15728644
  163.6 4.5 %copy-start.4 = (f32[512,512]{1,0:T(8,128)S(1)}, f32[512,512]{1,0:T(8,128)}, u32[]{:S(2)}) copy-start(f32[512,512]{1,0:T(8,128)} %param.15) | copy-start | bytes 3145732
  163.6 51.5 %all-to-all-start.1 = ((bf16[8,32,8,512]{3,2,1,0:T(8,128)(2,1)}), bf16[8,32,8,512]{3,2,1,0:T(8,128)(2,1)}, u32[]{:S(2)}, u32[]{:S(2)}) async-start(bf16[8,32,8,512]{3,2,1,0:T(8,128)(2,1)} %bitcast.9), calls=%async_computation.2 | async-start | bytes 4194304 | tf_op jit(solution)/shard_map/all_to_all | solution.py:312
  168.0 1.4 copy-start.7
  215.0 1.2 copy-start.3
  231.2 52.0 %all-to-all-start.2 = ((bf16[8,32,8,512]{3,2,1,0:T(8,128)(2,1)}), bf16[8,32,8,512]{3,2,1,0:T(8,128)(2,1)S(1)}, u32[]{:S(2)}, u32[]{:S(2)}) async-start(bf16[8,32,8,512]{3,2,1,0:T(8,128)(2,1)} %modes.1), calls=%async_computation.3 | async-start | bytes 4194304 | tf_op jit(solution)/shard_map/all_to_all | solution.py:312
  234.8 108.1 %all-gather.3.cloned.1.call-start = ((), (), s32[]{:S(2)}) async-start(), calls=%async_computation.6 | async-start | bytes 10485760 | tf_op jit(solution)/shard_map/all_gather | solution.py:343
  237.9 2.3 copy-start.1
  285.3 119.7 %all-to-all-start.3 = ((bf16[8,40,16,512]{3,2,1,0:T(8,128)(2,1)}), bf16[8,40,16,512]{3,2,1,0:T(8,128)(2,1)}, u32[]{:S(2)}, u32[]{:S(2)}) async-start(bf16[8,40,16,512]{3,2,1,0:T(8,128)(2,1)} %bitcast.30), calls=%async_computation.4 | async-start | bytes 10485760 | tf_op jit(solution)/shard_map/all_to_all | solution.py:312
  307.1 2.4 copy-start.2
Sparse Core Ops, SparseCore 0:
  21.7 74.3 reduce-scatter.1
  285.4 57.4 all-gather.2

commit v4 on v3

--- a/solution.py
+++ b/solution.py
@@ -139,7 +139,7 @@
         out_ref[s] = contrib_ref[source_ref[s]]
         return carry
 
-    lax.fori_loop(0, out_ref.shape[0], step, 0, unroll=4)
+    lax.fori_loop(0, out_ref.shape[0], step, 0, unroll=8)
     if len(refs) == 2:
         table_ref = refs[0]
         per_owner = out_ref.shape[0] // table_ref.shape[0]
@@ -179,7 +179,7 @@
 
         return carry
 
-    lax.fori_loop(0, values_ref.shape[0], step, 0, unroll=4)
+    lax.fori_loop(0, values_ref.shape[0], step, 0, unroll=8)
 
 
 def deposit(target, values, block_count):
@@ -244,7 +244,7 @@
 
         return carry
 
-    lax.fori_loop(0, values_ref.shape[0], step, 0, unroll=4)
+    lax.fori_loop(0, values_ref.shape[0], step, 0, unroll=8)
 
 
 def finish(target, values, base):

time: 425 us -> 424 us (level)
  transfers between devices with their start and end apart: 5 -> 5, of which waited for: 4 -> 4; matrix products, arithmetic and copies ran while one was open for 4% -> 4% of each run, Pallas kernels for 7% -> 6%
where the time goes in v4:
time: 424 us; the launch traced here: 423 us
  waiting for transfers between devices  171 us (40%)
  blocking collectives  126 us (30%)
  Pallas kernels  65.3 us (15%)
  local copies, waits for them, and re-layouts  27 us (6%)
  between operations  13.7 us (3%)
  starting transfers between devices  13 us (3%)
    all_to_all x3, waiting for transfers between devices, exchange(): lax.all_to_all(values, 'wide', split_axis=0, concat_axis=0, tiled=True)  137 us
    all_to_all x1, blocking collectives, exchange(): lax.all_to_all(values, 'wide', split_axis=0, concat_axis=0, tiled=True)  126 us
    all_gather x1, waiting for transfers between devices, shards(): lax.all_gather(synth.reshape(per_set, lat_dev, channels).transpose(1, 0,...  33.6 us
    pallas_call x1, Pallas kernels, modes(): pl.pallas_call(modes_body, grid_spec=pltpu.PrefetchScalarGridSpec(num_sca...  14.9 us
    optimization_barrier x2, local copies, waits for them, and re-layouts, shards(): lax.optimization_barrier((summed, first_recv, source))  13.5 us
    pallas_call x1, Pallas kernels, synthesis(): pl.pallas_call(synthesis_body, grid=(lat_dev,), in_specs=[pl.BlockSpec(tr...  13.2 us
    all_to_all x3, starting transfers between devices, exchange(): lax.all_to_all(values, 'wide', split_axis=0, concat_axis=0, tiled=True)  12.9 us
    pallas_call x1, Pallas kernels, finish(): pl.pallas_call(finish_body, grid_spec=pltpu.PrefetchScalarGridSpec(num_sc...  11.7 us
  transfers between devices with their start and end apart: 5, of which 4 were waited for; matrix products, arithmetic and copies ran while one was open for 4% of the time, Pallas kernels for 6%

profile of v4, /device:TPU:0, one launch (start us, length us, event | category | flops | bytes accessed | tf_op | source)
XLA Modules:
  0.0 423.4 jit_solution(17095356232630603049)
XLA Ops:
  10.0 11.5 %analysis.1 = bf16[4,8,256,512]{3,2,1,0:T(8,128)(2,1)} custom-call(bf16[1024,640]{1,0:T(8,128)(2,1)S(1)} %copy.29.trig_ref, bf16[8,640,512]{2,1,0:T(8,128)(2,1)} %grid_ref.1), custom_call_target="tpu_custom_call" | custom-call | flops 5368709120 | bytes 14942208 | tf_op jit(solution)/shard_map/analysis/pallas_call | solution.py:48
  22.7 1.5 copy.30
  24.3 4.0 convolution_convert_fusion.contrib_ref
  28.4 4.0 pack.2
  33.5 126.0 %all_to_all.20 = bf16[8,41,16,512]{3,2,1,0:T(8,128)(2,1)} all-to-all(bf16[8,41,16,512]{3,2,1,0:T(8,128)(2,1)} %bitcast.34), channel_id=1, replica_groups=mesh['wide'=8,'narrow'=4] {'wide'}, dimensions={0} | all-to-all | bytes 10747904 | tf_op jit(solution)/shard_map/all_to_all | solution.py:312
  159.5 4.1 copy.32
  163.6 4.5 %all-to-all-start.1 = ((bf16[8,32,8,512]{3,2,1,0:T(8,128)(2,1)}), bf16[8,32,8,512]{3,2,1,0:T(8,128)(2,1)}, u32[]{:S(2)}, u32[]{:S(2)}) async-start(bf16[8,32,8,512]{3,2,1,0:T(8,128)(2,1)} %bitcast.9), calls=%async_computation.2 | async-start | bytes 4194304 | tf_op jit(solution)/shard_map/all_to_all | solution.py:312
  168.1 1.3 convert_element_type.54.back_ref
  169.7 45.3 %all-to-all-done.1.fourier_ref = bf16[8,32,8,512]{3,2,1,0:T(8,128)(2,1)} async-done(((bf16[8,32,8,512]{3,2,1,0:T(8,128)(2,1)}), bf16[8,32,8,512]{3,2,1,0:T(8,128)(2,1)}, u32[]{:S(2)}, u32[]{:S(2)}) %all-to-all-start.1) | async-done | bytes 2097184 | tf_op jit(solution)/shard_map/all_to_all | solution.py:312
  215.0 1.2 copy-done.3
  216.3 14.9 %modes.1 = bf16[8,32,8,512]{3,2,1,0:T(8,128)(2,1)} custom-call(s32[16]{0:T(128)S(1)} %dynamic-slice_bitcast_fusion.wave_ref, bf16[16,64,512]{2,1,0:T(8,128)(2,1)S(1)} %copy-done.3, bf16[8,32,8,512]{3,2,1,0:T(8,128)(2,1)} %all-to-all-done.1.fourier_ref, bf16[512,512]{1,0:T(8,128)(2,1)S(1)} %convert_element_type.53.proj_ref, ...), custom_call_target="tpu_custom_call" | custom-call | flops 4294967296 | bytes 7340032 | tf_op jit(solution)/shard_map/modes/pallas_call | solution.py:111
  231.2 3.6 all-to-all-start.2
  234.8 2.8 pack.3
  237.7 2.3 copy-done.1
  240.0 43.2 %all-to-all-done.2 = bf16[8,32,8,512]{3,2,1,0:T(8,128)(2,1)S(1)} async-done(((bf16[8,32,8,512]{3,2,1,0:T(8,128)(2,1)}), bf16[8,32,8,512]{3,2,1,0:T(8,128)(2,1)S(1)}, u32[]{:S(2)}, u32[]{:S(2)}) %all-to-all-start.2) | async-done | bytes 2097184 | tf_op jit(solution)/shard_map/all_to_all | solution.py:312
  283.2 2.0 copy.35
  285.3 4.9 %all-to-all-start.3 = ((bf16[8,40,16,512]{3,2,1,0:T(8,128)(2,1)}), bf16[8,40,16,512]{3,2,1,0:T(8,128)(2,1)}, u32[]{:S(2)}, u32[]{:S(2)}) async-start(bf16[8,40,16,512]{3,2,1,0:T(8,128)(2,1)} %bitcast.30), calls=%async_computation.4 | async-start | bytes 10485760 | tf_op jit(solution)/shard_map/all_to_all | solution.py:312
  290.1 9.5 %copy.31 = bf16[8,41,16,512]{3,0,2,1:T(8,128)(2,1)S(1)} copy(bf16[8,41,16,512]{3,2,1,0:T(8,128)(2,1)} %all_to_all.20) | data formatting | bytes 10747904 | tf_op jit(solution)/shard_map/optimization_barrier | solution.py:326
  299.8 7.1 %deposit.1.first_ref = f32[160,16,512]{2,1,0:T(8,128)S(1)} custom-call(s32[328]{0:T(512)S(1)} %reshape.111.target_ref, bf16[328,16,512]{2,1,0:T(8,128)(2,1)} %bitcast.33), custom_call_target="tpu_custom_call" | custom-call | flops 2686976 | bytes 10616832 | tf_op jit(solution)/shard_map/deposit/pallas_call | solution.py:187
  306.8 2.4 copy-done.2
  309.2 33.6 %all-gather.3.cloned.1.call-done = bf16[32,256,512]{2,1,0:T(8,128)(2,1)} async-done(((bf16[8,256,512]{2,1,0:T(8,128)(2,1)}), bf16[32,256,512]{2,1,0:T(8,128)(2,1)}) %all-gather.3.cloned.1.call-update) | async-done | bytes 8388624 | tf_op jit(solution)/shard_map/all_gather | solution.py:343
  342.9 13.2 %synthesis.1.base_ref = f32[160,32,512]{2,1,0:T(8,128)} custom-call(bf16[640,1024]{1,0:T(8,128)(2,1)S(1)} %bitcast.32, bf16[4,8,256,512]{3,2,1,0:T(8,128)(2,1)} %bitcast.35, f32[160,16,512]{2,1,0:T(8,128)} %copy-done.2), custom_call_target="tpu_custom_call" | custom-call | flops 5368709120 | bytes 25427968 | tf_op jit(solution)/shard_map/synthesis/pallas_call | solution.py:216
  356.1 48.8 %all-to-all-done.3 = bf16[8,40,16,512]{3,2,1,0:T(8,128)(2,1)} async-done(((bf16[8,40,16,512]{3,2,1,0:T(8,128)(2,1)}), bf16[8,40,16,512]{3,2,1,0:T(8,128)(2,1)}, u32[]{:S(2)}, u32[]{:S(2)}) %all-to-all-start.3) | async-done | bytes 5242912 | tf_op jit(solution)/shard_map/all_to_all | solution.py:312
  404.9 11.7 %finish.1 = f32[160,32,512]{2,1,0:T(8,128)} custom-call(s32[320]{0:T(512)S(1)} %reshape.109.target_ref, bf16[320,16,512]{2,1,0:T(8,128)(2,1)} %bitcast.11.values_ref, f32[160,32,512]{2,1,0:T(8,128)} %synthesis.1.base_ref), custom_call_target="tpu_custom_call", output_to_operand_aliasing={{}: (2, {})} | custom-call | flops 2621440 | bytes 15728640 | tf_op jit(solution)/shard_map/finish/pallas_call | solution.py:255
  (49 shorter events, 6.3 us)
Async XLA Ops:
  6.5 152.9 %reduce-scatter.2.cloned.1.call-start = ((), (), s32[]{:S(2)}) async-start(), calls=%async_computation.5 | async-start | bytes 10485760 | tf_op jit(solution)/shard_map/reduce_scatter | solution.py:325
  21.5 0.7 copy-start.6
  21.5 0.9 copy-start.8
  21.5 1.2 copy-start.5
  28.4 5.1 %copy-start = (bf16[160,32,512]{2,1,0:T(8,128)(2,1)}, bf16[160,32,512]{2,1,0:T(8,128)(2,1)S(1)}, u32[]{:S(2)}) copy-start(bf16[160,32,512]{2,1,0:T(8,128)(2,1)S(1)} %convolution_convert_fusion.contrib_ref) | copy-start | bytes 15728644
  163.6 4.5 %copy-start.4 = (f32[512,512]{1,0:T(8,128)S(1)}, f32[512,512]{1,0:T(8,128)}, u32[]{:S(2)}) copy-start(f32[512,512]{1,0:T(8,128)} %param.15) | copy-start | bytes 3145732
  163.6 51.5 %all-to-all-start.1 = ((bf16[8,32,8,512]{3,2,1,0:T(8,128)(2,1)}), bf16[8,32,8,512]{3,2,1,0:T(8,128)(2,1)}, u32[]{:S(2)}, u32[]{:S(2)}) async-start(bf16[8,32,8,512]{3,2,1,0:T(8,128)(2,1)} %bitcast.9), calls=%async_computation.2 | async-start | bytes 4194304 | tf_op jit(solution)/shard_map/all_to_all | solution.py:312
  168.0 1.4 copy-start.7
  215.0 1.2 copy-start.3
  231.2 52.0 %all-to-all-start.2 = ((bf16[8,32,8,512]{3,2,1,0:T(8,128)(2,1)}), bf16[8,32,8,512]{3,2,1,0:T(8,128)(2,1)S(1)}, u32[]{:S(2)}, u32[]{:S(2)}) async-start(bf16[8,32,8,512]{3,2,1,0:T(8,128)(2,1)} %modes.1), calls=%async_computation.3 | async-start | bytes 4194304 | tf_op jit(solution)/shard_map/all_to_all | solution.py:312
  234.8 108.1 %all-gather.3.cloned.1.call-start = ((), (), s32[]{:S(2)}) async-start(), calls=%async_computation.6 | async-start | bytes 10485760 | tf_op jit(solution)/shard_map/all_gather | solution.py:343
  237.7 2.3 copy-start.1
  285.3 119.7 %all-to-all-start.3 = ((bf16[8,40,16,512]{3,2,1,0:T(8,128)(2,1)}), bf16[8,40,16,512]{3,2,1,0:T(8,128)(2,1)}, u32[]{:S(2)}, u32[]{:S(2)}) async-start(bf16[8,40,16,512]{3,2,1,0:T(8,128)(2,1)} %bitcast.30), calls=%async_computation.4 | async-start | bytes 10485760 | tf_op jit(solution)/shard_map/all_to_all | solution.py:312
  306.8 2.4 copy-start.2
Sparse Core Ops, SparseCore 0:
  21.7 74.3 reduce-scatter.1
  285.4 57.4 all-gather.2
